TPU v7x, 32 devices: a whole 2x2x4 slice. The times are simulated.
32 devices in a mesh: groups: 2 (over y), tensor: 4 (over z), dp: 4 (over x, core).
Axes of the slice: x: 2, y: 2, z: 4, core: 2. Of those that a mesh axis runs over, the one named last changes fastest.
Arguments:
- hidden_in: bfloat16 [512, 8192], P(('groups', 'dp'), 'tensor'), parts along dimension 0, may hold values from -6 to 6
- norm_gain: bfloat16 [8192], replicated, may hold values from 0.099609375 to 1.8984375
- w_query: bfloat16 [8192, 4096], P(None, 'tensor'), may hold values from -0.0625 to 0.0625
- w_keyval: bfloat16 [8192, 1024], P(None, 'tensor'), may hold values from -0.0625 to 0.0625
- w_out: bfloat16 [4096, 8192], P('tensor'), may hold values from -1 to 1
- kv_cache: bfloat16 [8, 64, 2048, 1024], P(('groups', 'dp'), 'tensor'), parts along dimension 0, may hold values from -305 to 305
- cache_length: int32 [512], P(('groups', 'dp')), parts along dimension 0, may hold values from 1 to 2048, as said below
- row_tenant: int32 [512], P(('groups', 'dp')), parts along dimension 0, may hold values from 0 to 799, as said below
- tenant_lists: int32 [8, 4, 8], P('groups'), parts along dimension 0, may hold values from -1 to 199, as said below
- adapter_heads: bfloat16 [800, 32, 4, 2, 512], P('dp', 'tensor'), may hold values from -6 to 6
- adapter_shared: bfloat16 [800, 16384], P('dp', 'tensor'), may hold values from -6 to 6
Outputs:
- attn_branch: bfloat16 [512, 8192], P(('groups', 'dp'), 'tensor'), parts along dimension 0
There are 2 independent parts, one for each index of `groups`. A program takes and returns all parts, laid end to end along the dimension named above; an argument that names none is the same for every part. Nothing has to cross between parts.
Inputs may be any that keep to these rules, and one draw needn't show every extreme that they name: `tenant_lists`: tenant s * 200 + k is the k-th tenant of store shard s. The entries of one list are distinct; its -1 entries stand at its end and it holds one entry or more. In every draw one data group gets 8 tenants from every store shard. `row_tenant`: row n belongs to data group n // 64. Every row's tenant is listed for its group by its store shard, and every listed tenant is the tenant of some row of that group. `cache_length`: some row has 2048 live positions.
All inputs are finite; a program needn't handle non-finite values.
Results may differ from a plain program's by a relative error of at most 0.012.
The roundings to bfloat16 on the way count: a program that leaves them out, or rounds other values in their place, can miss the bound.
Values may be sent and summed in bfloat16 or wider, within the bound.
A program may use at most 256 MiB of HBM per device.

v0:
```python
import math

import jax
import jax.numpy as jnp
from jax import lax
from jax.sharding import PartitionSpec as P

D = 8192
QH = 32
KVH = 4
HD = 128
I1 = 512
J1 = 16
RANK = 4


FLOOR_SCORE = -1e30
OUT_SCALE = 8.0


def select_rows(selector, table):
    flat = table.reshape(selector.shape[1], -1)
    return jnp.dot(selector, flat, preferred_element_type=jnp.float32).astype(jnp.bfloat16)


def fetch_factors(adapter_heads, adapter_shared, tenant_lists, row_tenant):
    groups = tenant_lists.shape[0]
    slots = tenant_lists.shape[2]
    stored = adapter_heads.shape[0]
    outgoing = lax.dynamic_index_in_dim(
        tenant_lists, lax.axis_index("dp"), 0, keepdims=False
    ).reshape(-1)
    picker = (outgoing[:, None] == jnp.arange(stored, dtype=jnp.int32)[None, :]).astype(
        jnp.bfloat16
    )
    send_heads = select_rows(picker, adapter_heads).reshape(
        (groups, slots) + adapter_heads.shape[1:]
    )
    send_shared = select_rows(picker, adapter_shared).reshape(
        groups, slots, adapter_shared.shape[1]
    )
    got_heads, got_shared = (
        lax.all_to_all(send_heads, "dp", split_axis=0, concat_axis=0, tiled=True),
        lax.all_to_all(send_shared, "dp", split_axis=0, concat_axis=0, tiled=True),
    )
    incoming = lax.dynamic_index_in_dim(tenant_lists, lax.axis_index("dp"), 1, keepdims=False)
    slot_ids = jnp.where(
        incoming >= 0, jnp.arange(groups, dtype=jnp.int32)[:, None] * stored + incoming, -1
    )
    selector = (row_tenant[:, None] == slot_ids.reshape(1, -1)).astype(jnp.bfloat16)
    head_rows = select_rows(selector, got_heads).reshape(
        (row_tenant.shape[0],) + adapter_heads.shape[1:]
    )
    return (selector, head_rows, got_shared)


def on_device(
    hidden_in,
    norm_gain,
    w_query,
    w_keyval,
    w_out,
    kv_cache,
    cache_length,
    row_tenant,
    tenant_lists,
    adapter_heads,
    adapter_shared,
):
    whole = lax.all_gather(hidden_in, "tensor", axis=1, tiled=True)
    row_count = whole.shape[0]
    heads_here = w_query.shape[1] // HD
    group_size = QH // KVH
    widened = whole.astype(jnp.float32)
    inverse = lax.rsqrt(jnp.mean(widened * widened, axis=1, keepdims=True) + 1e-05)
    normed = (widened * inverse * norm_gain.astype(jnp.float32)).astype(jnp.bfloat16)
    selector, head_rows, got_shared = fetch_factors(
        adapter_heads, adapter_shared, tenant_lists, row_tenant
    )
    blocks = normed.reshape(row_count, I1, J1)
    inner = jnp.einsum(
        "nhri,nij->nhrj", head_rows[:, :, :, 0, :], blocks, preferred_element_type=jnp.float32
    ).astype(jnp.bfloat16)
    base_query = jnp.dot(normed, w_query, preferred_element_type=jnp.float32)
    keyval = jnp.dot(normed, w_keyval, preferred_element_type=jnp.float32).astype(jnp.bfloat16)
    query_coeff = 1.0 / math.sqrt(RANK * D)
    rows_here = kv_cache.shape[1]
    span = kv_cache.shape[2]
    first_row = lax.axis_index("tensor") * rows_here
    everyone = lax.all_gather(got_shared, "tensor", axis=2, tiled=True)
    shared_rows = select_rows(selector, everyone)
    query_factor = shared_rows[:, : RANK * J1 * HD].reshape(row_count, RANK, J1, HD)
    query_delta = jnp.einsum(
        "nhrj,nrje->nhe", inner, query_factor, preferred_element_type=jnp.float32
    ).reshape(row_count, heads_here * HD)
    query = (base_query + query_coeff * query_delta).astype(jnp.bfloat16)
    queries, fresh = (
        lax.all_to_all(query, "tensor", split_axis=0, concat_axis=1, tiled=True),
        lax.all_to_all(keyval, "tensor", split_axis=0, concat_axis=1, tiled=True),
    )
    lengths = lax.dynamic_slice_in_dim(cache_length, first_row, rows_here, 0)
    score_coeff = 1.0 / math.sqrt(HD)
    full_width = KVH * 2 * HD
    cache_flat = kv_cache.reshape(rows_here, span, full_width)
    columns = jnp.arange(full_width, dtype=jnp.int32)
    head_group = jnp.arange(QH, dtype=jnp.int32) // group_size
    same_group = columns[None, :] // (2 * HD) == head_group[:, None]
    key_cols = same_group & (columns[None, :] // HD % 2 == 0)
    value_cols = same_group & (columns[None, :] // HD % 2 == 1)
    query_heads = queries.reshape(rows_here, QH, HD)
    spread_query = jnp.tile(query_heads, (1, 1, 2 * KVH))
    spread_query = jnp.where(key_cols[None, :, :], spread_query, jnp.zeros_like(spread_query))
    scores = (
        jnp.einsum("rhc,rpc->rhp", spread_query, cache_flat, preferred_element_type=jnp.float32)
        * score_coeff
    )
    visible = jnp.arange(span, dtype=jnp.int32)[None, :] < lengths[:, None]
    scores = jnp.where(visible[:, None, :], scores, FLOOR_SCORE)
    own_score = (
        jnp.einsum("rhc,rc->rh", spread_query, fresh, preferred_element_type=jnp.float32)
        * score_coeff
    )
    peak = jnp.maximum(jnp.max(scores, axis=2), own_score)
    expo = jnp.exp(scores - peak[:, :, None])
    expo_new = jnp.exp(own_score - peak)
    totals = jnp.sum(expo, axis=2) + expo_new
    weights = expo.astype(jnp.bfloat16)
    weight_new = lax.optimization_barrier(expo_new.astype(jnp.bfloat16)).astype(jnp.float32)
    summed_wide = jnp.einsum(
        "rhp,rpc->rhc", weights, cache_flat, preferred_element_type=jnp.float32
    )
    summed_wide = summed_wide + weight_new[:, :, None] * fresh.astype(jnp.float32)[:, None, :]
    summed_wide = jnp.where(value_cols[None, :, :], summed_wide, 0.0)
    summed = jnp.sum(summed_wide.reshape(rows_here, QH, 2 * KVH, HD), axis=2)
    attended_rows = (summed / totals[:, :, None]).astype(jnp.bfloat16).reshape(rows_here, QH * HD)
    attended = lax.all_to_all(attended_rows, "tensor", split_axis=1, concat_axis=0, tiled=True)
    heads_view = attended.reshape(row_count, heads_here, HD)
    out_factor = shared_rows[:, RANK * J1 * HD :].reshape(row_count, RANK, HD, J1)
    mixed_factor = jnp.einsum(
        "nhe,nrej->nhrj", heads_view, out_factor, preferred_element_type=jnp.float32
    ).astype(jnp.bfloat16)
    out_delta = jnp.einsum(
        "nhrj,nhri->nij", mixed_factor, head_rows[:, :, :, 1, :], preferred_element_type=jnp.float32
    ).reshape(row_count, D)
    out_coeff = OUT_SCALE / math.sqrt(RANK * QH * HD)
    partial_value = (
        jnp.dot(attended, w_out, preferred_element_type=jnp.float32) + out_coeff * out_delta
    ).astype(jnp.bfloat16)
    summed_out = lax.psum_scatter(partial_value, "tensor", scatter_dimension=1, tiled=True).astype(
        jnp.float32
    )
    return summed_out.astype(jnp.bfloat16)


def solution(mesh):
    placed = (
        P(("groups", "dp"), "tensor"),
        P(),
        P(None, "tensor"),
        P(None, "tensor"),
        P("tensor", None),
        P(("groups", "dp"), "tensor", None, None),
        P(("groups", "dp")),
        P(("groups", "dp")),
        P("groups", None, None),
        P("dp", "tensor", None, None, None),
        P("dp", "tensor"),
    )
    return jax.shard_map(
        on_device,
        mesh=mesh,
        in_specs=placed,
        out_specs=P(("groups", "dp"), "tensor"),
        check_vma=False,
    )
```

profile of v0, /device:TPU:9, one launch (start us, length us, event | category | flops | bytes accessed | tf_op | source)
XLA Modules:
  0.0 275.3 jit_solution(4704437203392863061)
XLA Ops:
  9.2 4.1 %all-to-all-start.1 = ((bf16[4,8,4096]{2,1,0:T(8,128)(2,1)}), bf16[4,8,4096]{2,1,0:T(8,128)(2,1)S(1)}, u32[]{:S(2)}, u32[]{:S(2)}) async-start(bf16[4,8,4096]{2,1,0:T(8,128)(2,1)} %fusion.5), calls=%async_computation.1 | async-start | bytes 524288 | tf_op jit(solution)/shard_map/all_to_all | solution.py:44
  13.9 22.1 %reshape.310 = bf16[200,32768]{1,0:T(8,128)(2,1)} reshape(bf16[200,8,4,2,512]{4,3,2,1,0:T(2,128)(2,1)} %param.20) | data formatting | bytes 26214400 | tf_op jit(solution)/shard_map/reshape | solution.py:22
  36.0 8.7 %convolution_convert_fusion.1 = bf16[32,32768]{1,0:T(8,128)(2,1)} fusion(bf16[200,32768]{1,0:T(8,128)(2,1)} %reshape.310, s32[32]{0:T(128)S(1)} %eq.83), kind=kOutput, calls=%fused_computation.5 | convolution fusion | flops 420485376 | bytes 15204480 | tf_op jit(solution)/shard_map/dot_general | solution.py:23
  44.8 4.6 %all-to-all-start = ((bf16[4,8,8,4,2,512]{5,1,4,3,2,0:T(8,128)(2,1)}), bf16[4,8,8,4,2,512]{5,1,4,3,2,0:T(8,128)(2,1)}, u32[]{:S(2)}, u32[]{:S(2)}) async-start(bf16[4,8,8,4,2,512]{5,1,4,3,2,0:T(8,128)(2,1)} %bitcast.95), calls=%async_computation | async-start | bytes 4194304 | tf_op jit(solution)/shard_map/all_to_all | solution.py:43
  50.7 23.6 %all-to-all-done = bf16[4,8,8,4,2,512]{5,1,4,3,2,0:T(8,128)(2,1)} async-done(((bf16[4,8,8,4,2,512]{5,1,4,3,2,0:T(8,128)(2,1)}), bf16[4,8,8,4,2,512]{5,1,4,3,2,0:T(8,128)(2,1)}, u32[]{:S(2)}, u32[]{:S(2)}) %all-to-all-start) | async-done | bytes 2097184 | tf_op jit(solution)/shard_map/all_to_all | solution.py:43
  74.3 4.8 %convolution_convert_fusion = bf16[64,32768]{1,0:T(8,128)(2,1)} fusion(bf16[32,32768]{1,0:T(8,128)(2,1)} %bitcast.1, s32[32]{0:T(128)S(1)} %compare_select_fusion, s32[64]{0:T(128)S(1)} %copy-done.4), kind=kOutput, calls=%fused_computation.4 | convolution fusion | flops 136316928 | bytes 6291840 | tf_op jit(solution)/shard_map/dot_general | solution.py:23
  79.1 7.8 %reshape.313 = bf16[64,8,4,2,512]{4,3,2,1,0:T(2,128)(2,1)} reshape(bf16[64,32768]{1,0:T(8,128)(2,1)} %convolution_convert_fusion) | data formatting | bytes 8388608 | tf_op jit(solution)/shard_map/reshape | solution.py:51
  86.9 1.5 fusion.9
  88.5 1.5 fusion.11
  90.0 1.8 copy.35
  91.8 4.3 %copy.45 = bf16[64,512,16,1]{1,2,3,0:T(8,128)(2,1)} copy(bf16[64,512,16,1]{0,2,1,3:T(8,128)(2,1)} %bitcast.97) | data formatting | bytes 2097152 | tf_op jit(solution)/shard_map/reshape | solution.py:80
  96.1 3.6 %convolution_convert_fusion.5 = bf16[64,256]{1,0:T(8,128)(2,1)} fusion(bf16[64,8192]{1,0:T(8,128)(2,1)S(1)} %fusion.11, bf16[8192,256]{1,0:T(8,128)(2,1)} %param.14), kind=kOutput, calls=%fused_computation.39 | convolution fusion | flops 268451840 | bytes 5275648 | tf_op jit(solution)/shard_map/dot_general | solution.py:85
  99.7 4.8 %all-to-all-start.3 = ((bf16[4,16,256]{2,1,0:T(8,128)(2,1)}), bf16[4,16,256]{2,1,0:T(8,128)(2,1)S(1)}, u32[]{:S(2)}, u32[]{:S(2)}) async-start(bf16[4,16,256]{2,1,0:T(8,128)(2,1)} %bitcast.12), calls=%async_computation.3 | async-start | bytes 65536 | tf_op jit(solution)/shard_map/all_to_all | solution.py:99
  104.5 11.2 %fusion.54 = (bf16[64,8,4,1,512]{4,3,2,1,0:T(2,128)(2,1)}, bf16[64,8,4,1,512]{4,3,2,1,0:T(2,128)(2,1)}) fusion(bf16[64,8,4,2,512]{4,3,2,1,0:T(2,128)(2,1)} %reshape.313), kind=kLoop, calls=%fused_computation.95 | loop fusion | bytes 8388608 | tf_op jit(solution)/shard_map/slice | solution.py:82
  115.7 2.0 convolution_convert_fusion.2
  117.8 1.2 copy.56
  119.1 4.7 %fusion.26 = f32[64,8,128]{2,1,0:T(8,128)S(1)} fusion(bf16[64,4,16,128]{3,2,1,0:T(8,128)(2,1)} %bitcast.101, bf16[64,512,16,1]{1,2,3,0:T(8,128)(2,1)} %copy.45, bf16[64,8,4,1,512]{4,3,2,1,0:T(2,128)(2,1)} %get-tuple-element.5), kind=kOutput, calls=%fused_computation.37 | convolution fusion | flops 42041344 | bytes 4456448 | tf_op jit(solution)/shard_map/nhrj,nrje->nhe/dot_general | solution.py:93
  123.8 9.5 %fusion.27 = bf16[64,1024]{1,0:T(8,128)(2,1)} fusion(bf16[64,8192]{1,0:T(8,128)(2,1)S(1)} %fusion.11, bf16[8192,1024]{1,0:T(8,128)(2,1)} %param.13, f32[8,8,8,128]{3,2,1,0:T(8,128)S(1)} %bitcast.106), kind=kOutput, calls=%fused_computation.38 | convolution fusion | flops 1073872896 | bytes 18219008 | tf_op jit(solution)/shard_map/dot_general | solution.py:84
  133.2 4.5 %all-to-all-start.2 = ((bf16[4,16,1024]{2,1,0:T(8,128)(2,1)}), bf16[4,16,1024]{2,1,0:T(8,128)(2,1)S(1)}, u32[]{:S(2)}, u32[]{:S(2)}) async-start(bf16[4,16,1024]{2,1,0:T(8,128)(2,1)} %bitcast.9), calls=%async_computation.2 | async-start | bytes 262144 | tf_op jit(solution)/shard_map/all_to_all | solution.py:98
  137.9 4.1 %all-to-all-done.2 = bf16[4,16,1024]{2,1,0:T(8,128)(2,1)S(1)} async-done(((bf16[4,16,1024]{2,1,0:T(8,128)(2,1)}), bf16[4,16,1024]{2,1,0:T(8,128)(2,1)S(1)}, u32[]{:S(2)}, u32[]{:S(2)}) %all-to-all-start.2) | async-done | bytes 131104 | tf_op jit(solution)/shard_map/all_to_all | solution.py:98
  143.4 1.5 tile.12
  145.3 29.5 %fusion.6 = (f32[16,32]{1,0:T(8,128)S(1)}, f32[16,32,2048]{2,1,0:T(8,128)}) fusion(pred[16,2048]{1,0:T(8,128)(4,1)S(1)} %iota_compare_fusion, bf16[1,16,2048,1024]{3,2,1,0:T(8,128)(2,1)} %param.16, bf16[16,32,1024]{2,1,0:T(8,128)(2,1)S(1)} %tile.12, pred[32,1024]{1,0:T(8,128)(4,1)S(1)} %get-tuple-element.12), kind=kOutput, calls=%fused_computation.13 | convolution fusion | flops 2151153152 | bytes 72419328 | tf_op jit(solution)/shard_map/rhc,rpc->rhp/dot_general | solution.py:114
  174.8 3.4 %fusion.7 = f32[16,32]{1,0:T(8,128)S(1)} fusion(f32[16,32,2048]{2,1,0:T(8,128)} %get-tuple-element.14, f32[16,32]{1,0:T(8,128)S(1)} %multiply_maximum_fusion, pred[16,2048]{1,0:T(8,128)(4,1)S(1)} %iota_compare_fusion), kind=kLoop, calls=%fused_computation.14 | loop fusion | flops 4193792 | bytes 4231168 | tf_op jit(solution)/shard_map/reduce_sum | solution.py:126
  178.2 24.6 %add_select_fusion = f32[16,32,1024]{2,1,0:T(8,128)S(1)} fusion(bf16[1,16,2048,1024]{3,2,1,0:T(8,128)(2,1)} %param.16, f32[16,32,2048]{2,1,0:T(8,128)} %get-tuple-element.14, f32[16,32]{1,0:T(8,128)S(1)} %multiply_maximum_fusion, pred[16,2048]{1,0:T(8,128)(4,1)S(1)} %iota_compare_fusion, f32[16,1024]{1,0:T(8,128)S(1)} %convert_element_type.77, ...), kind=kOutput, calls=%fused_computation.27 | convolution fusion | flops 2153250816 | bytes 73535488 | tf_op jit(solution)/shard_map/rhp,rpc->rhc/dot_general | solution.py:129
  204.6 3.8 %all-to-all-start.4 = ((bf16[16,4,1024]{2,0,1:T(8,128)(2,1)}), bf16[16,4,1024]{2,0,1:T(8,128)(2,1)S(1)}, u32[]{:S(2)}, u32[]{:S(2)}) async-start(bf16[16,4,1024]{2,0,1:T(8,128)(2,1)} %copy.39), calls=%async_computation.4 | async-start | bytes 262144 | tf_op jit(solution)/shard_map/all_to_all | solution.py:136
  208.4 1.8 copy.41
  210.2 3.9 %copy.42 = bf16[64,4,128,16]{2,3,1,0:T(8,128)(2,1)S(1)} copy(bf16[64,4,128,16]{0,3,2,1:T(8,128)(2,1)} %bitcast.96) | data formatting | bytes 2097152 | tf_op jit(solution)/shard_map/reshape | solution.py:138
  214.2 7.2 %bitcast_multiply_fusion = f32[64,512,16]{1,2,0:T(8,128)} fusion(bf16[64,8,4,1,512]{4,3,2,1,0:T(2,128)(2,1)} %get-tuple-element.6, bf16[64,4,128,16]{2,3,1,0:T(8,128)(2,1)S(1)} %copy.42, bf16[64,8,128,1]{2,1,0,3:T(8,128)(2,1)S(1)} %bitcast.103), kind=kOutput, calls=%fused_computation.26 | convolution fusion | flops 42500096 | bytes 5373952 | tf_op jit(solution)/shard_map/nhrj,nhri->nij/dot_general | solution.py:142
  221.4 5.2 %copy.43 = f32[64,512,16]{0,2,1:T(8,128)} copy(f32[64,512,16]{1,2,0:T(8,128)} %bitcast_multiply_fusion) | data formatting | bytes 4194304 | tf_op jit(solution)/shard_map/mul | solution.py:147
  226.6 3.8 %copy.44 = f32[64,8192]{1,0:T(8,128)} copy(f32[64,8192]{0,1:T(8,128)} %bitcast.93) | data formatting | bytes 4194304 | tf_op jit(solution)/shard_map/mul | solution.py:147
  230.5 10.5 %fusion.4 = bf16[64,8192]{1,0:T(8,128)(2,1)} fusion(f32[64,8192]{1,0:T(8,128)} %copy.44, bf16[64,1024]{1,0:T(8,128)(2,1)S(1)} %bitcast.100, bf16[1024,8192]{1,0:T(8,128)(2,1)} %param.15), kind=kOutput, calls=%fused_computation.8 | convolution fusion | flops 1074790400 | bytes 20054016 | tf_op jit(solution)/shard_map/dot_general | solution.py:147
  241.0 27.8 %reduce-scatter.2.cloned.1.call-done = bf16[64,2048]{1,0:T(8,128)(2,1)} async-done(((bf16[64,8192]{1,0:T(8,128)(2,1)}), bf16[64,2048]{1,0:T(8,128)(2,1)}) %reduce-scatter.2.cloned.1.call-update) | async-done | bytes 262160 | tf_op jit(solution)/shard_map/reduce_scatter | solution.py:149
  (58 shorter events, 8.6 us)
Async XLA Ops:
  6.5 1.4 copy-start
  9.2 35.6 %all-to-all-start.1 = ((bf16[4,8,4096]{2,1,0:T(8,128)(2,1)}), bf16[4,8,4096]{2,1,0:T(8,128)(2,1)S(1)}, u32[]{:S(2)}, u32[]{:S(2)}) async-start(bf16[4,8,4096]{2,1,0:T(8,128)(2,1)} %fusion.5), calls=%async_computation.1 | async-start | bytes 524288 | tf_op jit(solution)/shard_map/all_to_all | solution.py:44
  13.2 73.7 %all-gather.3.cloned.1.call-start = ((), (), s32[]{:S(2)}) async-start(), calls=%async_computation.6 | async-start | bytes 1310720 | tf_op jit(solution)/shard_map/all_gather | solution.py:70
  44.8 5.6 %copy-start.3 = (bf16[8192]{0:T(1024)(128)(2,1)S(1)}, bf16[8192]{0:T(1024)(128)(2,1)}, u32[]{:S(2)}) copy-start(bf16[8192]{0:T(1024)(128)(2,1)} %param.12) | copy-start | bytes 49156
  44.8 5.6 %copy-start.5 = (s32[64]{0:T(128)S(1)}, s32[64]{0:T(128)}, u32[]{:S(2)}) copy-start(s32[64]{0:T(128)} %param.17) | copy-start | bytes 772
  44.8 29.5 %copy-start.4 = (s32[64]{0:T(128)S(1)}, s32[64]{0:T(128)}, u32[]{:S(2)}) copy-start(s32[64]{0:T(128)} %param.18) | copy-start | bytes 772
  44.8 5.8 %copy-start.2 = (bf16[4,8,4096]{2,1,0:T(8,128)(2,1)}, bf16[4,8,4096]{2,1,0:T(8,128)(2,1)S(1)}, u32[]{:S(2)}) copy-start(bf16[4,8,4096]{2,1,0:T(8,128)(2,1)S(1)} %all-to-all-done.1) | copy-start | bytes 786436
  44.8 29.5 %all-to-all-start = ((bf16[4,8,8,4,2,512]{5,1,4,3,2,0:T(8,128)(2,1)}), bf16[4,8,8,4,2,512]{5,1,4,3,2,0:T(8,128)(2,1)}, u32[]{:S(2)}, u32[]{:S(2)}) async-start(bf16[4,8,8,4,2,512]{5,1,4,3,2,0:T(8,128)(2,1)} %bitcast.95), calls=%async_computation | async-start | bytes 4194304 | tf_op jit(solution)/shard_map/all_to_all | solution.py:43
  49.4 66.3 %all-gather.5.cloned.1.call-start = ((), (), s32[]{:S(2)}) async-start(), calls=%async_computation.7 | async-start | bytes 1310720 | tf_op jit(solution)/shard_map/all_gather | solution.py:90
  99.7 33.5 %all-to-all-start.3 = ((bf16[4,16,256]{2,1,0:T(8,128)(2,1)}), bf16[4,16,256]{2,1,0:T(8,128)(2,1)S(1)}, u32[]{:S(2)}, u32[]{:S(2)}) async-start(bf16[4,16,256]{2,1,0:T(8,128)(2,1)} %bitcast.12), calls=%async_computation.3 | async-start | bytes 65536 | tf_op jit(solution)/shard_map/all_to_all | solution.py:99
  133.2 8.8 %all-to-all-start.2 = ((bf16[4,16,1024]{2,1,0:T(8,128)(2,1)}), bf16[4,16,1024]{2,1,0:T(8,128)(2,1)S(1)}, u32[]{:S(2)}, u32[]{:S(2)}) async-start(bf16[4,16,1024]{2,1,0:T(8,128)(2,1)} %bitcast.9), calls=%async_computation.2 | async-start | bytes 262144 | tf_op jit(solution)/shard_map/all_to_all | solution.py:98
  204.6 9.5 %all-to-all-start.4 = ((bf16[16,4,1024]{2,0,1:T(8,128)(2,1)}), bf16[16,4,1024]{2,0,1:T(8,128)(2,1)S(1)}, u32[]{:S(2)}, u32[]{:S(2)}) async-start(bf16[16,4,1024]{2,0,1:T(8,128)(2,1)} %copy.39), calls=%async_computation.4 | async-start | bytes 262144 | tf_op jit(solution)/shard_map/all_to_all | solution.py:136
  208.4 60.4 %reduce-scatter.2.cloned.1.call-start = ((), (), s32[]{:S(2)}) async-start(), calls=%async_computation.8 | async-start | bytes 1310720 | tf_op jit(solution)/shard_map/reduce_scatter | solution.py:149
  230.5 38.3 %copy-start.1 = (bf16[200,4096]{1,0:T(8,128)(2,1)S(1)}, bf16[200,4096]{1,0:T(8,128)(2,1)}, u32[]{:S(2)}) copy-start(bf16[200,4096]{1,0:T(8,128)(2,1)} %param.21) | copy-start | bytes 4915204
Sparse Core Ops, SparseCore 0:
  15.6 28.6 all-gather.2
  51.8 28.7 all-gather.4
  241.1 27.6 reduce-scatter.1
where the time goes:
time: 281 us; the launch traced here: 275 us
  matrix products  107 us (38%)
  local copies, waits for them, and re-layouts  70.1 us (25%)
  waiting for transfers between devices  56.3 us (20%)
  starting transfers between devices  21.7 us (8%)
  between operations  13.3 us (5%)
  other arithmetic  7.34 us (3%)
    dot_general x1, matrix products, on_device(): jnp.einsum('rhc,rpc->rhp', spread_query, cache_flat, preferred_element_ty...  29.5 us
    reduce_scatter x1, waiting for transfers between devices, on_device(): lax.psum_scatter(partial_value, 'tensor', scatter_dimension=1, tiled=True)  27.8 us
    dot_general x1, matrix products, on_device(): jnp.einsum('rhp,rpc->rhc', weights, cache_flat, preferred_element_type=jn...  24.6 us
    all_to_all x1, waiting for transfers between devices, fetch_factors(): lax.all_to_all(send_heads, 'dp', split_axis=0, concat_axis=0, tiled=True)  23.6 us
    reshape x1, local copies, waits for them, and re-layouts, select_rows(): flat = table.reshape(selector.shape[1], -1)  22.1 us
    dot_general x4, matrix products, select_rows(): jnp.dot(selector, flat, preferred_element_type=jnp.float32)  16.7 us
    slice x1, local copies, waits for them, and re-layouts, on_device(): head_rows[:, :, :, 0, :]  11.2 us
    dot_general x1, matrix products, on_device(): jnp.dot(attended, w_out, preferred_element_type=jnp.float32)  10.5 us
  transfers between devices with their start and end apart: 8, of which 3 were waited for; matrix products, arithmetic and copies ran while one was open for 33% of the time, Pallas kernels for 0%

commit v1 on v0

v1 whole, which is shorter than its diff:
```python
import functools
import math

import jax
import jax.numpy as jnp
from jax import lax
from jax.experimental import pallas as pl
from jax.experimental.pallas import tpu as pltpu
from jax.sharding import PartitionSpec as P

D = 8192
QH = 32
KVH = 4
HD = 128
I1 = 512
J1 = 16
RANK = 4
FLOOR_SCORE = -1e30
OUT_SCALE = 8.0
GRAIN = 256
F32 = jnp.float32
BF16 = jnp.bfloat16
VMEM_BYTES = 56 * 1024 * 1024


def params(**more):
    return pltpu.CompilerParams(vmem_limit_bytes=VMEM_BYTES, **more)


def nt_dot(left, right):
    return lax.dot_general(left, right, (((1,), (1,)), ((), ())), preferred_element_type=F32)


def pick_kernel(count, index_ref, store_ref, out_ref, sems):
    def start(k, carry):
        pltpu.make_async_copy(store_ref.at[index_ref[k]], out_ref.at[k], sems.at[k]).start()
        return carry

    def finish(k, carry):
        pltpu.make_async_copy(store_ref.at[0], out_ref.at[k], sems.at[k]).wait()
        return carry

    lax.fori_loop(0, count, start, 0)
    lax.fori_loop(0, count, finish, 0)


def pick_tenants(indices, store):
    count = indices.shape[0]
    return pl.pallas_call(
        functools.partial(pick_kernel, count),
        grid_spec=pltpu.PrefetchScalarGridSpec(
            num_scalar_prefetch=1,
            grid=(1,),
            in_specs=[pl.BlockSpec(memory_space=pl.ANY)],
            out_specs=pl.BlockSpec(memory_space=pl.ANY),
            scratch_shapes=[pltpu.SemaphoreType.DMA((count,))],
        ),
        out_shape=jax.ShapeDtypeStruct((count,) + store.shape[1:], store.dtype),
        compiler_params=params(),
    )(indices, store)


def project_kernel(depth, hidden_ref, gain_ref, wq_ref, wkv_ref, normed_ref, base_ref, keyval_ref, acc):
    step = pl.program_id(0)

    @pl.when(step == 0)
    def _():
        wide = hidden_ref[...].astype(F32)
        inverse = lax.rsqrt(jnp.mean(wide * wide, axis=1, keepdims=True) + 1e-05)
        normed_ref[...] = (wide * inverse * gain_ref[...].astype(F32)).astype(BF16)
        base_ref[...] = jnp.zeros_like(base_ref)
        acc[...] = jnp.zeros_like(acc)

    part = normed_ref[:, pl.ds(pl.multiple_of(step * depth, depth), depth)]
    base_ref[...] += jnp.dot(part, wq_ref[...], preferred_element_type=F32)
    acc[...] += jnp.dot(part, wkv_ref[...], preferred_element_type=F32)

    @pl.when(step == pl.num_programs(0) - 1)
    def _():
        keyval_ref[...] = acc[...].astype(BF16)


def project(hidden, gain, w_query, w_keyval):
    rows = hidden.shape[0]
    depth = 1024
    q_cols, kv_cols = w_query.shape[1], w_keyval.shape[1]
    whole = lambda k: (0, 0)
    return pl.pallas_call(
        functools.partial(project_kernel, depth),
        grid=(D // depth,),
        in_specs=[
            pl.BlockSpec((rows, D), whole),
            pl.BlockSpec((1, D), whole),
            pl.BlockSpec((depth, q_cols), lambda k: (k, 0)),
            pl.BlockSpec((depth, kv_cols), lambda k: (k, 0)),
        ],
        out_specs=[
            pl.BlockSpec((rows, D), whole),
            pl.BlockSpec((rows, q_cols), whole),
            pl.BlockSpec((rows, kv_cols), whole),
        ],
        out_shape=[
            jax.ShapeDtypeStruct((rows, D), BF16),
            jax.ShapeDtypeStruct((rows, q_cols), F32),
            jax.ShapeDtypeStruct((rows, kv_cols), BF16),
        ],
        scratch_shapes=[pltpu.VMEM((rows, kv_cols), F32)],
        compiler_params=params(),
        cost_estimate=pl.CostEstimate(
            flops=2 * rows * D * (q_cols + kv_cols),
            bytes_accessed=2 * D * (q_cols + kv_cols),
            transcendentals=0,
        ),
    )(hidden, gain.reshape(1, D), w_query, w_keyval)


def query_kernel(heads, normed_ref, factor_ref, shared_ref, mask_ref, base_ref, query_ref, turned, spread, inner):
    rows = normed_ref.shape[0]
    lanes = mask_ref.shape[1]
    half = D // 2
    piece = half // 4
    for c in range(4):
        both = jnp.concatenate(
            [normed_ref[:, c * piece : (c + 1) * piece], normed_ref[:, half + c * piece : half + (c + 1) * piece]],
            axis=0,
        ).astype(F32)
        turned[c * piece : (c + 1) * piece, :] = both.T
    for j in range(J1):
        back = turned[pl.ds(j, I1 // 2, stride=J1), :].T
        spread[j * rows : (j + 1) * rows, : I1 // 2] = back[:rows].astype(BF16)
        spread[j * rows : (j + 1) * rows, I1 // 2 :] = back[rows:].astype(BF16)
    mask = mask_ref[...]
    for h in range(heads):
        factor = jnp.concatenate([factor_ref[s, h] for s in range(factor_ref.shape[0])], axis=0)
        for j0 in range(0, J1, 4):
            part = nt_dot(spread[j0 * rows : (j0 + 4) * rows, :], factor)
            for j in range(4):
                own = jnp.where(mask > 0, part[j * rows : (j + 1) * rows], 0.0)
                inner[j0 + j, h * rows : (h + 1) * rows, :] = own.astype(BF16)
    delta = jnp.zeros((heads * rows, HD), F32)
    for j in range(J1):
        delta += jnp.dot(inner[j], shared_ref[:, j * HD : (j + 1) * HD], preferred_element_type=F32)
    coeff = 1.0 / math.sqrt(RANK * D)
    for h in range(heads):
        cols = slice(h * HD, (h + 1) * HD)
        query_ref[:, cols] = (base_ref[:, cols] + coeff * delta[h * rows : (h + 1) * rows]).astype(BF16)


def adapt_query(normed, factors, shared, mask, base):
    rows, cols = base.shape
    heads = cols // HD
    return pl.pallas_call(
        functools.partial(query_kernel, heads),
        out_shape=jax.ShapeDtypeStruct((rows, cols), BF16),
        scratch_shapes=[
            pltpu.VMEM((D // 2, 2 * rows), F32),
            pltpu.VMEM((J1 * rows, I1), BF16),
            pltpu.VMEM((J1, heads * rows, mask.shape[1]), BF16),
        ],
        compiler_params=params(),
    )(normed, factors, shared, mask, base)


def attend_kernel(slots, length_ref, query_ref, fresh_ref, cache_ref, out_ref, held, scores, sems):
    rows, span = cache_ref.shape[0], cache_ref.shape[1]
    per_group = QH // KVH
    pieces = span // GRAIN
    coeff = 1.0 / math.sqrt(HD)

    def chunks_of(row):
        return (length_ref[row] + (GRAIN - 1)) // GRAIN

    def copy_of(row, c):
        slot = lax.rem(row, slots)
        where = pl.ds(pl.multiple_of(c * GRAIN, GRAIN), GRAIN)
        return pltpu.make_async_copy(
            cache_ref.at[row, where], held.at[slot, where], sems.at[slot, c]
        )

    def fetch(row):
        def one(c, carry):
            copy_of(row, c).start()
            return carry

        lax.fori_loop(0, chunks_of(row), one, 0)

    for row in range(min(slots - 1, rows)):
        fetch(row)

    def per_row(row, carry):
        @pl.when(row + slots - 1 < rows)
        def _():
            fetch(row + slots - 1)

        slot = lax.rem(row, slots)
        count = chunks_of(row)
        length = length_ref[row]
        query = query_ref[row]
        newest = fresh_ref[row].astype(F32)
        own_parts, value_parts = [], []
        for g in range(KVH):
            heads = slice(g * per_group, (g + 1) * per_group)
            key = newest[2 * g : 2 * g + 1]
            own_parts.append(jnp.sum(query[heads].astype(F32) * key, axis=1, keepdims=True))
            value_parts.append(jnp.broadcast_to(newest[2 * g + 1 : 2 * g + 2], (per_group, HD)))
        own = jnp.concatenate(own_parts, axis=0) * coeff
        value_new = jnp.concatenate(value_parts, axis=0)

        def finish(c, carry):
            copy_of(row, c).wait()
            return carry

        for n in range(1, pieces + 1):
            @pl.when(count == n)
            def _(n=n):
                for c in range(n):
                    finish(c, 0)
                    where = slice(c * GRAIN, (c + 1) * GRAIN)
                    for g in range(KVH):
                        heads = slice(g * per_group, (g + 1) * per_group)
                        keys = held[slot, where, 2 * g * HD : (2 * g + 1) * HD]
                        scores[heads, where] = nt_dot(query[heads], keys) * coeff
                width = n * GRAIN
                full = scores[:, :width]
                spot = lax.broadcasted_iota(jnp.int32, (QH, width), 1)
                full = jnp.where(spot < length, full, FLOOR_SCORE)
                peak = jnp.maximum(jnp.max(full, axis=1, keepdims=True), own)
                expo = jnp.exp(full - peak)
                expo_new = jnp.exp(own - peak)
                total = jnp.sum(expo, axis=1, keepdims=True) + expo_new
                weight = expo.astype(BF16)
                weight_new = expo_new.astype(BF16).astype(F32)
                summed = jnp.concatenate(
                    [
                        jnp.dot(
                            weight[g * per_group : (g + 1) * per_group],
                            held[slot, :width, (2 * g + 1) * HD : (2 * g + 2) * HD],
                            preferred_element_type=F32,
                        )
                        for g in range(KVH)
                    ],
                    axis=0,
                )
                out_ref[row] = ((summed + weight_new * value_new) / total).astype(BF16)

        return carry

    lax.fori_loop(0, rows, per_row, 0)


def attend(lengths, queries, fresh, cache):
    rows, span, width = cache.shape
    slots = min(4, rows + 1)
    return pl.pallas_call(
        functools.partial(attend_kernel, slots),
        in_specs=[
            pl.BlockSpec(memory_space=pltpu.SMEM),
            pl.BlockSpec(memory_space=pltpu.VMEM),
            pl.BlockSpec(memory_space=pltpu.VMEM),
            pl.BlockSpec(memory_space=pl.ANY),
        ],
        out_specs=pl.BlockSpec(memory_space=pltpu.VMEM),
        out_shape=jax.ShapeDtypeStruct((rows, QH, HD), BF16),
        scratch_shapes=[
            pltpu.VMEM((slots, span, width), BF16),
            pltpu.VMEM((QH, span), F32),
            pltpu.SemaphoreType.DMA((slots, span // GRAIN)),
        ],
        compiler_params=params(),
        cost_estimate=pl.CostEstimate(
            flops=4 * rows * span * QH * HD,
            bytes_accessed=rows * span * width,
            transcendentals=rows * span * QH,
        ),
    )(lengths, queries, fresh, cache)


def output_kernel(heads, att_ref, factor_ref, shared_ref, mask_ref, low_ref, high_ref, out_ref, turned, mixed, factors, spread):
    step = pl.program_id(0)
    rows = att_ref.shape[0]
    lanes = mask_ref.shape[1]
    width = low_ref.shape[1]
    half = I1 // 2

    @pl.when(step == 0)
    def _():
        for c in range(4):
            cols = slice(c * I1, (c + 1) * I1)
            turned[cols, :] = shared_ref[:, cols].astype(F32).T
        stack = jnp.concatenate([att_ref[:, h * HD : (h + 1) * HD] for h in range(heads)], axis=0)
        mask = mask_ref[...]
        for j in range(J1):
            table = turned[pl.ds(j, HD, stride=J1), :].astype(BF16)
            part = jnp.dot(stack, table, preferred_element_type=F32)
            for h in range(heads):
                own = jnp.where(mask > 0, part[h * rows : (h + 1) * rows], 0.0)
                mixed[j * rows : (j + 1) * rows, h * lanes : (h + 1) * lanes] = own.astype(BF16)
        sources = factor_ref.shape[0]
        depth = factor_ref.shape[2]
        for h in range(heads):
            for s in range(sources):
                first = h * lanes + s * depth
                factors[first : first + depth, :] = factor_ref[s, h]
        for j0 in range(0, J1, 4):
            delta = jnp.dot(mixed[j0 * rows : (j0 + 4) * rows, :], factors[...], preferred_element_type=F32)
            for j in range(4):
                own = delta[j * rows : (j + 1) * rows]
                both = jnp.concatenate([own[:, :half], own[:, half:]], axis=0)
                spread[pl.ds(j0 + j, half, stride=J1), :] = both.T

    coeff = OUT_SCALE / math.sqrt(RANK * QH * HD)
    delta = spread[pl.ds(pl.multiple_of(step * width, width), width), :].T
    att = att_ref[...]
    for side, weight in enumerate((low_ref, high_ref)):
        base = jnp.dot(att, weight[...], preferred_element_type=F32)
        out_ref[side] = (base + coeff * delta[side * rows : (side + 1) * rows]).astype(BF16)


def project_out(attended, factors, shared, mask, w_out):
    rows, inner = attended.shape
    heads = inner // HD
    lanes = mask.shape[1]
    width = 512
    steps = D // 2 // width
    whole2 = lambda k: (0, 0)
    out = pl.pallas_call(
        functools.partial(output_kernel, heads),
        grid=(steps,),
        in_specs=[
            pl.BlockSpec((rows, inner), whole2),
            pl.BlockSpec(factors.shape, lambda k: (0, 0, 0, 0)),
            pl.BlockSpec(shared.shape, whole2),
            pl.BlockSpec(mask.shape, whole2),
            pl.BlockSpec((inner, width), lambda k: (0, k)),
            pl.BlockSpec((inner, width), lambda k: (0, k + steps)),
        ],
        out_specs=pl.BlockSpec((2, rows, width), lambda k: (0, 0, k)),
        out_shape=jax.ShapeDtypeStruct((2, rows, D // 2), BF16),
        scratch_shapes=[
            pltpu.VMEM((J1 * HD, lanes), F32),
            pltpu.VMEM((J1 * rows, heads * lanes), BF16),
            pltpu.VMEM((heads * lanes, I1), BF16),
            pltpu.VMEM((D // 2, 2 * rows), F32),
        ],
        compiler_params=params(),
    )(attended, factors, shared, mask, w_out, w_out)
    return out


def on_device(
    hidden_in,
    norm_gain,
    w_query,
    w_keyval,
    w_out,
    kv_cache,
    cache_length,
    row_tenant,
    tenant_lists,
    adapter_heads,
    adapter_shared,
):
    groups, slots = tenant_lists.shape[0], tenant_lists.shape[2]
    stored, heads_here = adapter_heads.shape[:2]
    dp = lax.axis_index("dp")
    outgoing = lax.dynamic_index_in_dim(tenant_lists, dp, 0, keepdims=False).reshape(-1)

    hidden = lax.all_gather(hidden_in, "tensor", axis=1, tiled=True)
    picker = (outgoing[:, None] == jnp.arange(stored, dtype=jnp.int32)[None, :]).astype(BF16)
    send_shared = (
        jnp.dot(picker, adapter_shared, preferred_element_type=F32)
        .astype(BF16)
        .reshape(groups, slots, adapter_shared.shape[1])
    )
    got_shared = lax.all_to_all(send_shared, "dp", split_axis=0, concat_axis=0, tiled=True)
    everyone = lax.all_gather(got_shared, "tensor", axis=2, tiled=True)
    tables = everyone.reshape(groups * slots, 2, RANK, J1 * HD)
    lanes = groups * slots * RANK
    shared_query = tables[:, 0].reshape(lanes, J1 * HD)
    shared_out = tables[:, 1].reshape(lanes, J1 * HD)

    picked = pick_tenants(jnp.maximum(outgoing, 0), adapter_heads)
    picked = picked.reshape(groups, slots, heads_here, RANK, 2, I1)

    def exchange(part):
        send = picked[:, :, :, :, part, :].transpose(0, 2, 1, 3, 4)
        send = send.reshape(groups, heads_here, slots * RANK, I1)
        return lax.all_to_all(send, "dp", split_axis=0, concat_axis=0, tiled=True)

    heads_query = exchange(0)
    heads_out = exchange(1)

    incoming = lax.dynamic_index_in_dim(tenant_lists, dp, 1, keepdims=False)
    ids = jnp.where(incoming >= 0, jnp.arange(groups, dtype=jnp.int32)[:, None] * stored + incoming, -1)
    ids = jnp.repeat(ids.reshape(-1), RANK)
    mask = (row_tenant[:, None] == ids[None, :]).astype(F32)

    normed, base, keyval = project(hidden, norm_gain, w_query, w_keyval)
    query = adapt_query(normed, heads_query, shared_query, mask, base)

    rows_here, span, width = kv_cache.shape[1:]
    both = jnp.concatenate([query, keyval], axis=1)
    both = lax.all_to_all(both, "tensor", split_axis=0, concat_axis=0, tiled=True)
    parts = both.reshape(-1, rows_here, both.shape[1])
    q_cols = query.shape[1]
    queries = parts[:, :, :q_cols].transpose(1, 0, 2).reshape(rows_here, QH, HD)
    fresh = parts[:, :, q_cols:].transpose(1, 0, 2).reshape(rows_here, 2 * KVH, HD)
    first_row = lax.axis_index("tensor") * rows_here
    lengths = lax.dynamic_slice_in_dim(cache_length, first_row, rows_here, 0)
    attended = attend(lengths, queries, fresh, kv_cache.reshape(rows_here, span, width))
    attended = lax.all_to_all(
        attended.reshape(rows_here, QH * HD), "tensor", split_axis=1, concat_axis=0, tiled=True
    )
    partial = project_out(attended, heads_out, shared_out, mask, w_out)
    row_count = partial.shape[1]
    partial = partial.transpose(1, 0, 2).reshape(row_count, D)
    return lax.psum_scatter(partial, "tensor", scatter_dimension=1, tiled=True)


def solution(mesh):
    placed = (
        P(("groups", "dp"), "tensor"),
        P(),
        P(None, "tensor"),
        P(None, "tensor"),
        P("tensor", None),
        P(("groups", "dp"), "tensor", None, None),
        P(("groups", "dp")),
        P(("groups", "dp")),
        P("groups", None, None),
        P("dp", "tensor", None, None, None),
        P("dp", "tensor"),
    )
    return jax.shard_map(
        on_device,
        mesh=mesh,
        in_specs=placed,
        out_specs=P(("groups", "dp"), "tensor"),
        check_vma=False,
    )
```

time: 281 us -> 233 us (0.83)
  Pallas kernels: 0 us -> 125 us
  matrix products: 107 us -> 1.17 us
  local copies, waits for them, and re-layouts: 70.1 us -> 28.3 us
  waiting for transfers between devices: 56.3 us -> 38.6 us
  other arithmetic: 7.34 us -> 2.79 us
    pallas_call x0 -> x5, Pallas kernels: none -> 125 us  [the longest x1 65.6 us: pick_tenants(): pl.pallas_call(functools.partial(pick_kernel, count), grid_spec=pltpu.Pre...]
    dot_general x12 -> x1, matrix products: 107 us -> 1.17 us  [on_device(): jnp.dot(picker, adapter_shared, preferred_element_type=F32).astype(BF16)]
    reshape x4 -> x8, local copies, waits for them, and re-layouts: 38.2 us -> 9.23 us  [the longest x1 2.62 us: on_device(): tables = everyone.reshape(groups * slots, 2, RANK, J1 * HD)]
    all_to_all x5, waiting for transfers between devices: 27.7 us -> 5.54 us  [the longest x1 2.81 us: on_device(): lax.all_to_all(both, 'tensor', split_axis=0, concat_axis=0, tiled=True)]
    mul x2 -> x0, local copies, waits for them, and re-layouts: 9.09 us -> none  [on_device(): out_coeff * out_delta]
    reduce_sum x3 -> x0, other arithmetic: 5.41 us -> none  [the longest x1 3.35 us: on_device(): totals = jnp.sum(expo, axis=2) + expo_new]
    slice x2, local copies, waits for them, and re-layouts: 13 us -> 8.51 us  [the longest x1 5.87 us: exchange(): send = picked[:, :, :, :, part, :].transpose(0, 2, 1, 3, 4)]
  transfers between devices with their start and end apart: 8 -> 8, of which waited for: 3 -> 4; matrix products, arithmetic and copies ran while one was open for 33% -> 11% of each run, Pallas kernels for 0% -> 46%
where the time goes in v1:
time: 233 us; the launch traced here: 229 us
  Pallas kernels  125 us (54%)
  waiting for transfers between devices  38.6 us (17%)
  local copies, waits for them, and re-layouts  28.3 us (12%)
  starting transfers between devices  20.2 us (9%)
  between operations  13.2 us (6%)
  other arithmetic  2.79 us (1%)
    pallas_call x1, Pallas kernels, pick_tenants(): pl.pallas_call(functools.partial(pick_kernel, count), grid_spec=pltpu.Pre...  65.6 us
    reduce_scatter x1, waiting for transfers between devices, on_device(): return lax.psum_scatter(partial, 'tensor', scatter_dimension=1, tiled=True)  29.6 us
    pallas_call x1, Pallas kernels, attend(): pl.pallas_call(functools.partial(attend_kernel, slots), in_specs=[pl.Bloc...  26.5 us
    pallas_call x1, Pallas kernels, project_out(): pl.pallas_call(functools.partial(output_kernel, heads), grid=(steps,), in...  13.7 us
    pallas_call x1, Pallas kernels, project(): pl.pallas_call(functools.partial(project_kernel, depth), grid=(D // depth...  12.6 us
    all_to_all x2, starting transfers between devices, exchange(): return lax.all_to_all(send, 'dp', split_axis=0, concat_axis=0, tiled=True)  9.06 us
    pallas_call x1, Pallas kernels, adapt_query(): pl.pallas_call(functools.partial(query_kernel, heads), out_shape=jax.Shap...  6.6 us
    slice x1, local copies, waits for them, and re-layouts, exchange(): send = picked[:, :, :, :, part, :].transpose(0, 2, 1, 3, 4)  5.87 us
  transfers between devices with their start and end apart: 8, of which 4 were waited for; matrix products, arithmetic and copies ran while one was open for 11% of the time, Pallas kernels for 46%

profile of v1, /device:TPU:9, one launch (start us, length us, event | category | flops | bytes accessed | tf_op | source)
XLA Modules:
  0.0 229.2 jit_solution(13820454443528336146)
XLA Ops:
  6.5 0.7 all-gather.3.cloned.1.call-update
  7.3 0.7 constant_dynamic-slice_fusion
  8.0 1.2 fusion
  9.2 4.0 %all-to-all-start.1 = ((bf16[4,8,4096]{2,1,0:T(8,128)(2,1)}), bf16[4,8,4096]{2,1,0:T(8,128)(2,1)S(1)}, u32[]{:S(2)}, u32[]{:S(2)}) async-start(bf16[4,8,4096]{2,1,0:T(8,128)(2,1)} %fusion), calls=%async_computation.1 | async-start | bytes 524288 | tf_op jit(solution)/shard_map/all_to_all | solution.py:375
  13.8 65.6 %shard_map.110 = bf16[32,8,4,2,512]{4,3,2,1,0:T(2,128)(2,1)} custom-call(s32[32]{0:T(128)} %broadcast_maximum_fusion.index_ref, bf16[200,8,4,2,512]{4,3,2,1,0:T(2,128)(2,1)} %store_ref.1), custom_call_target="tpu_custom_call" | custom-call | tf_op jit(solution)/shard_map/pallas_call | solution.py:49
  79.4 0.7 copy-done.5
  80.1 5.9 %fusion.2 = (bf16[4,8,8,4,1,512]{5,4,3,2,1,0:T(2,128)(2,1)S(1)}, bf16[4,8,8,4,1,512]{5,4,3,2,1,0:T(2,128)(2,1)S(1)}) fusion(bf16[4,8,8,4,2,512]{5,4,3,2,1,0:T(2,128)(2,1)} %bitcast.26), kind=kLoop, calls=%fused_computation.15 | loop fusion | bytes 4194304 | tf_op jit(solution)/shard_map/slice | solution.py:386
  86.6 1.1 reshape.58
  87.7 3.6 %all-to-all-start = ((bf16[4,8,32,512]{3,2,1,0:T(8,128)(2,1)}), bf16[4,8,32,512]{3,2,1,0:T(8,128)(2,1)S(1)}, u32[]{:S(2)}, u32[]{:S(2)}) async-start(bf16[4,8,32,512]{3,2,1,0:T(8,128)(2,1)} %reshape.58), calls=%async_computation | async-start | bytes 2097152 | tf_op jit(solution)/shard_map/all_to_all | solution.py:388
  91.3 0.7 dynamic-slice_reduce_fusion
  93.7 12.6 %shard_map.109 = (bf16[64,8192]{1,0:T(8,128)(2,1)}, f32[64,1024]{1,0:T(8,128)}, bf16[64,256]{1,0:T(8,128)(2,1)}) custom-call(bf16[64,8192]{1,0:T(8,128)(2,1)} %all-gather.3.cloned.1.call-done.hidden_ref, bf16[1,8192]{1,0:T(2,128)(2,1)} %reshape.55.gain_ref, bf16[8192,1024]{1,0:T(8,128)(2,1)} %wq_ref.1, bf16[8192,256]{1,0:T(8,128)(2,1)} %wkv_ref.1), custom_call_target="tpu_custom_call" | custom-call | flops 1342177280 | bytes 20971520 | tf_op jit(solution)/shard_map/pallas_call | solution.py:88
  106.3 2.7 %all-gather.5.cloned.1.call-done = bf16[4,8,16384]{2,1,0:T(8,128)(2,1)} async-done(((bf16[4,8,4096]{2,1,0:T(8,128)(2,1)}), bf16[4,8,16384]{2,1,0:T(8,128)(2,1)}) %all-gather.5.cloned.1.call-update) | async-done | bytes 1048592 | tf_op jit(solution)/shard_map/all_gather | solution.py:376
  109.0 2.6 %reshape.60 = bf16[32,2,4,2048]{3,2,1,0:T(4,128)(2,1)} reshape(bf16[4,8,16384]{2,1,0:T(8,128)(2,1)} %all-gather.5.cloned.1.call-done) | data formatting | bytes 2097152 | tf_op jit(solution)/shard_map/reshape | solution.py:377
  111.6 2.6 %fusion.3 = (bf16[32,1,4,2048]{3,2,1,0:T(4,128)(2,1)}, bf16[32,1,4,2048]{3,2,1,0:T(4,128)(2,1)}) fusion(bf16[32,2,4,2048]{3,2,1,0:T(4,128)(2,1)} %reshape.60), kind=kLoop, calls=%fused_computation.16 | loop fusion | bytes 2097152 | tf_op jit(solution)/shard_map/slice | solution.py:380
  114.2 2.0 reshape_squeeze.6.shared_ref
  116.2 0.9 copy-done.2
  117.2 6.6 %shard_map.111 = bf16[64,1024]{1,0:T(8,128)(2,1)} custom-call(bf16[64,8192]{1,0:T(8,128)(2,1)} %get-tuple-element.8.normed_ref, bf16[4,8,32,512]{3,2,1,0:T(8,128)(2,1)} %copy-done.2, bf16[128,2048]{1,0:T(8,128)(2,1)} %reshape_squeeze.6.shared_ref, f32[64,128]{1,0:T(8,128)} %compare_convert_fusion.mask_ref, f32[64,1024]{1,0:T(8,128)} %get-tuple-element.9.base_ref), custom_call_target="tpu_custom_call" | custom-call | tf_op jit(solution)/shard_map/pallas_call | solution.py:152
  123.8 1.6 pad_maximum_fusion
  125.4 3.7 %all-to-all-start.2 = ((bf16[4,16,1280]{2,1,0:T(8,128)(2,1)}), bf16[4,16,1280]{2,1,0:T(8,128)(2,1)S(1)}, u32[]{:S(2)}, u32[]{:S(2)}) async-start(bf16[4,16,1280]{2,1,0:T(8,128)(2,1)} %bitcast.4), calls=%async_computation.2 | async-start | bytes 327680 | tf_op jit(solution)/shard_map/all_to_all | solution.py:403
  129.6 1.2 reshape.64
  130.8 2.8 %all-to-all-done.2 = bf16[4,16,1280]{2,1,0:T(8,128)(2,1)S(1)} async-done(((bf16[4,16,1280]{2,1,0:T(8,128)(2,1)}), bf16[4,16,1280]{2,1,0:T(8,128)(2,1)S(1)}, u32[]{:S(2)}, u32[]{:S(2)}) %all-to-all-start.2) | async-done | bytes 163872 | tf_op jit(solution)/shard_map/all_to_all | solution.py:403
  133.6 5.5 %all-to-all-start.4 = ((bf16[4,8,32,512]{3,2,1,0:T(8,128)(2,1)}), bf16[4,8,32,512]{3,2,1,0:T(8,128)(2,1)S(1)}, u32[]{:S(2)}, u32[]{:S(2)}) async-start(bf16[4,8,32,512]{3,2,1,0:T(8,128)(2,1)} %reshape.64), calls=%async_computation.4 | async-start | bytes 2097152 | tf_op jit(solution)/shard_map/all_to_all | solution.py:388
  139.8 0.7 reshape.61.query_ref
  141.2 26.5 %shard_map.112 = bf16[16,32,128]{2,1,0:T(8,128)(2,1)} custom-call(s32[16]{0:T(128)} %dynamic_slice.11.length_ref, bf16[16,32,128]{2,1,0:T(8,128)(2,1)} %reshape.61.query_ref, bf16[16,8,128]{2,1,0:T(8,128)(2,1)} %reshape.62.fresh_ref, bf16[16,2048,1024]{2,1,0:T(8,128)(2,1)} %bitcast.7.cache_ref), custom_call_target="tpu_custom_call" | custom-call | flops 536870912 | bytes 33554432 | tf_op jit(solution)/shard_map/pallas_call | solution.py:254
  167.7 0.9 all_to_all.33
  168.6 0.7 copy.24
  169.3 3.3 %all-to-all-start.3 = ((bf16[16,4,1024]{2,0,1:T(8,128)(2,1)}), bf16[16,4,1024]{2,0,1:T(8,128)(2,1)S(1)}, u32[]{:S(2)}, u32[]{:S(2)}) async-start(bf16[16,4,1024]{2,0,1:T(8,128)(2,1)} %copy.24), calls=%async_computation.3 | async-start | bytes 262144 | tf_op jit(solution)/shard_map/all_to_all | solution.py:411
  172.7 0.9 reshape_squeeze.7.shared_ref
  173.6 2.7 %all-to-all-done.3 = bf16[16,4,1024]{2,0,1:T(8,128)(2,1)S(1)} async-done(((bf16[16,4,1024]{2,0,1:T(8,128)(2,1)}), bf16[16,4,1024]{2,0,1:T(8,128)(2,1)S(1)}, u32[]{:S(2)}, u32[]{:S(2)}) %all-to-all-start.3) | async-done | bytes 131104 | tf_op jit(solution)/shard_map/all_to_all | solution.py:411
  177.0 13.7 %shard_map.113 = bf16[2,64,4096]{2,1,0:T(8,128)(2,1)} custom-call(bf16[64,1024]{1,0:T(8,128)(2,1)} %bitcast.31, bf16[4,8,32,512]{3,2,1,0:T(8,128)(2,1)} %copy-done.3, bf16[128,2048]{1,0:T(8,128)(2,1)} %reshape_squeeze.7.shared_ref, f32[64,128]{1,0:T(8,128)} %compare_convert_fusion.mask_ref, bf16[1024,8192]{1,0:T(8,128)(2,1)} %high_ref.1, ...), custom_call_target="tpu_custom_call" | custom-call | tf_op jit(solution)/shard_map/pallas_call | solution.py:326
  190.7 2.3 %copy.29 = bf16[2,8,8,4096]{3,2,0,1:T(8,128)(2,1)} copy(bf16[2,8,8,4096]{3,2,1,0:T(8,128)(2,1)} %bitcast.30) | data formatting | bytes 2097152 | tf_op jit(solution)/shard_map/reshape | solution.py:416
  193.0 29.6 %reduce-scatter.2.cloned.1.call-done = bf16[64,2048]{1,0:T(8,128)(2,1)} async-done(((bf16[64,8192]{1,0:T(8,128)(2,1)}), bf16[64,2048]{1,0:T(8,128)(2,1)}) %reduce-scatter.2.cloned.1.call-update) | async-done | bytes 262160 | tf_op jit(solution)/shard_map/reduce_scatter | solution.py:417
  (48 shorter events, 5.6 us)
Async XLA Ops:
  6.5 1.5 copy-start
  6.5 87.2 %all-gather.3.cloned.1.call-start = ((), (), s32[]{:S(2)}) async-start(), calls=%async_computation.6 | async-start | bytes 1310720 | tf_op jit(solution)/shard_map/all_gather | solution.py:368
  9.2 70.2 %all-to-all-start.1 = ((bf16[4,8,4096]{2,1,0:T(8,128)(2,1)}), bf16[4,8,4096]{2,1,0:T(8,128)(2,1)S(1)}, u32[]{:S(2)}, u32[]{:S(2)}) async-start(bf16[4,8,4096]{2,1,0:T(8,128)(2,1)} %fusion), calls=%async_computation.1 | async-start | bytes 524288 | tf_op jit(solution)/shard_map/all_to_all | solution.py:375
  13.3 95.7 %all-gather.5.cloned.1.call-start = ((), (), s32[]{:S(2)}) async-start(), calls=%async_computation.7 | async-start | bytes 1310720 | tf_op jit(solution)/shard_map/all_gather | solution.py:376
  79.4 0.7 copy-start.5
  86.6 5.8 %copy-start.8 = (bf16[8192]{0:T(1024)(128)(2,1)S(1)}, bf16[8192]{0:T(1024)(128)(2,1)}, u32[]{:S(2)}) copy-start(bf16[8192]{0:T(1024)(128)(2,1)} %param.12) | copy-start | bytes 49156
  86.6 6.5 %copy-start.9 = (s32[64]{0:T(128)S(1)}, s32[64]{0:T(128)}, u32[]{:S(2)}) copy-start(s32[64]{0:T(128)} %param.18) | copy-start | bytes 772
  87.7 28.5 %all-to-all-start = ((bf16[4,8,32,512]{3,2,1,0:T(8,128)(2,1)}), bf16[4,8,32,512]{3,2,1,0:T(8,128)(2,1)S(1)}, u32[]{:S(2)}, u32[]{:S(2)}) async-start(bf16[4,8,32,512]{3,2,1,0:T(8,128)(2,1)} %reshape.58), calls=%async_computation | async-start | bytes 2097152 | tf_op jit(solution)/shard_map/all_to_all | solution.py:388
  114.2 9.5 %copy-start.7 = (bf16[64,256]{1,0:T(8,128)(2,1)S(1)}, bf16[64,256]{1,0:T(8,128)(2,1)}, u32[]{:S(2)}) copy-start(bf16[64,256]{1,0:T(8,128)(2,1)} %get-tuple-element.10) | copy-start | bytes 98308
  116.2 0.9 copy-start.2
  125.4 8.3 %all-to-all-start.2 = ((bf16[4,16,1280]{2,1,0:T(8,128)(2,1)}), bf16[4,16,1280]{2,1,0:T(8,128)(2,1)S(1)}, u32[]{:S(2)}, u32[]{:S(2)}) async-start(bf16[4,16,1280]{2,1,0:T(8,128)(2,1)} %bitcast.4), calls=%async_computation.2 | async-start | bytes 327680 | tf_op jit(solution)/shard_map/all_to_all | solution.py:403
  129.6 9.5 %copy-start.10 = (s32[64]{0:T(128)S(1)}, s32[64]{0:T(128)}, u32[]{:S(2)}) copy-start(s32[64]{0:T(128)} %param.17) | copy-start | bytes 772
  133.6 35.7 %all-to-all-start.4 = ((bf16[4,8,32,512]{3,2,1,0:T(8,128)(2,1)}), bf16[4,8,32,512]{3,2,1,0:T(8,128)(2,1)S(1)}, u32[]{:S(2)}, u32[]{:S(2)}) async-start(bf16[4,8,32,512]{3,2,1,0:T(8,128)(2,1)} %reshape.64), calls=%async_computation.4 | async-start | bytes 2097152 | tf_op jit(solution)/shard_map/all_to_all | solution.py:388
  141.2 31.5 %copy-start.4 = (bf16[32,1,4,2048]{3,2,1,0:T(4,128)(2,1)S(1)}, bf16[32,1,4,2048]{3,2,1,0:T(4,128)(2,1)}, u32[]{:S(2)}) copy-start(bf16[32,1,4,2048]{3,2,1,0:T(4,128)(2,1)} %get-tuple-element.13) | copy-start | bytes 1572868
  169.3 7.0 %copy-start.3 = (bf16[4,8,32,512]{3,2,1,0:T(8,128)(2,1)}, bf16[4,8,32,512]{3,2,1,0:T(8,128)(2,1)S(1)}, u32[]{:S(2)}) copy-start(bf16[4,8,32,512]{3,2,1,0:T(8,128)(2,1)S(1)} %all-to-all-done.4.factor_ref) | copy-start | bytes 3145732
  169.3 7.0 %all-to-all-start.3 = ((bf16[16,4,1024]{2,0,1:T(8,128)(2,1)}), bf16[16,4,1024]{2,0,1:T(8,128)(2,1)S(1)}, u32[]{:S(2)}, u32[]{:S(2)}) async-start(bf16[16,4,1024]{2,0,1:T(8,128)(2,1)} %copy.24), calls=%async_computation.3 | async-start | bytes 262144 | tf_op jit(solution)/shard_map/all_to_all | solution.py:411
  172.7 50.0 %reduce-scatter.2.cloned.1.call-start = ((), (), s32[]{:S(2)}) async-start(), calls=%async_computation.8 | async-start | bytes 1310720 | tf_op jit(solution)/shard_map/reduce_scatter | solution.py:417
  176.4 0.7 copy-start.6
  177.0 45.6 %copy-start.1 = (bf16[200,4096]{1,0:T(8,128)(2,1)S(1)}, bf16[200,4096]{1,0:T(8,128)(2,1)}, u32[]{:S(2)}) copy-start(bf16[200,4096]{1,0:T(8,128)(2,1)} %param.21) | copy-start | bytes 4915204
Sparse Core Ops, SparseCore 0:
  8.9 28.8 all-gather.2
  80.2 28.6 all-gather.4
  193.2 29.4 reduce-scatter.1

commit v2 on v1

--- a/solution.py
+++ b/solution.py
@@ -32,29 +32,22 @@
 
 
 def pick_kernel(count, index_ref, store_ref, out_ref, sems):
-    def start(k, carry):
+    for k in range(count):
         pltpu.make_async_copy(store_ref.at[index_ref[k]], out_ref.at[k], sems.at[k]).start()
-        return carry
-
-    def finish(k, carry):
-        pltpu.make_async_copy(store_ref.at[0], out_ref.at[k], sems.at[k]).wait()
-        return carry
-
-    lax.fori_loop(0, count, start, 0)
-    lax.fori_loop(0, count, finish, 0)
+    for k in range(count):
+        pltpu.make_async_copy(store_ref.at[index_ref[k]], out_ref.at[k], sems.at[k]).wait()
 
 
 def pick_tenants(indices, store):
     count = indices.shape[0]
     return pl.pallas_call(
         functools.partial(pick_kernel, count),
-        grid_spec=pltpu.PrefetchScalarGridSpec(
-            num_scalar_prefetch=1,
-            grid=(1,),
-            in_specs=[pl.BlockSpec(memory_space=pl.ANY)],
-            out_specs=pl.BlockSpec(memory_space=pl.ANY),
-            scratch_shapes=[pltpu.SemaphoreType.DMA((count,))],
-        ),
+        in_specs=[
+            pl.BlockSpec(memory_space=pltpu.SMEM),
+            pl.BlockSpec(memory_space=pl.ANY),
+        ],
+        out_specs=pl.BlockSpec(memory_space=pltpu.VMEM),
+        scratch_shapes=[pltpu.SemaphoreType.DMA((count,))],
         out_shape=jax.ShapeDtypeStruct((count,) + store.shape[1:], store.dtype),
         compiler_params=params(),
     )(indices, store)
@@ -275,76 +268,190 @@
     )(lengths, queries, fresh, cache)
 
 
-def output_kernel(heads, att_ref, factor_ref, shared_ref, mask_ref, low_ref, high_ref, out_ref, turned, mixed, factors, spread):
-    step = pl.program_id(0)
-    rows = att_ref.shape[0]
-    lanes = mask_ref.shape[1]
-    width = low_ref.shape[1]
+def output_kernel(
+    devices,
+    att_ref,
+    factor_ref,
+    shared_ref,
+    mask_ref,
+    weight_ref,
+    out_ref,
+    weights,
+    got_att,
+    flat_att,
+    turned,
+    mixed,
+    factors,
+    spread,
+    delta_rows,
+    leaving,
+    arriving,
+    weight_sems,
+    att_send,
+    att_recv,
+    sum_send,
+    sum_recv,
+):
+    me = lax.axis_index("tensor")
+    heads, rows_here = att_ref.shape[1], att_ref.shape[2]
+    rows, lanes = mask_ref.shape
+    width = weights.shape[2]
     half = I1 // 2
 
-    @pl.when(step == 0)
-    def _():
-        for c in range(4):
-            cols = slice(c * I1, (c + 1) * I1)
-            turned[cols, :] = shared_ref[:, cols].astype(F32).T
-        stack = jnp.concatenate([att_ref[:, h * HD : (h + 1) * HD] for h in range(heads)], axis=0)
-        mask = mask_ref[...]
-        for j in range(J1):
-            table = turned[pl.ds(j, HD, stride=J1), :].astype(BF16)
-            part = jnp.dot(stack, table, preferred_element_type=F32)
-            for h in range(heads):
-                own = jnp.where(mask > 0, part[h * rows : (h + 1) * rows], 0.0)
-                mixed[j * rows : (j + 1) * rows, h * lanes : (h + 1) * lanes] = own.astype(BF16)
-        sources = factor_ref.shape[0]
-        depth = factor_ref.shape[2]
+    def other(k):
+        return lax.rem(me + k, devices)
+
+    def weight_copy(k):
+        where = pl.ds(pl.multiple_of(other(k) * width, width), width)
+        return pltpu.make_async_copy(weight_ref.at[:, where], weights.at[k], weight_sems.at[k])
+
+    def att_copy(k):
+        return pltpu.make_async_remote_copy(
+            src_ref=att_ref.at[other(k)],
+            dst_ref=got_att.at[me],
+            send_sem=att_send.at[k],
+            recv_sem=att_recv.at[me],
+            device_id={"tensor": other(k)},
+            device_id_type=pl.DeviceIdType.MESH,
+        )
+
+    def att_arrival(k):
+        return pltpu.make_async_remote_copy(
+            src_ref=att_ref.at[other(k)],
+            dst_ref=got_att.at[other(k)],
+            send_sem=att_send.at[k],
+            recv_sem=att_recv.at[other(k)],
+            device_id={"tensor": other(k)},
+            device_id_type=pl.DeviceIdType.MESH,
+        )
+
+    def sum_copy(k):
+        return pltpu.make_async_remote_copy(
+            src_ref=leaving.at[k],
+            dst_ref=arriving.at[me],
+            send_sem=sum_send.at[k],
+            recv_sem=sum_recv.at[me],
+            device_id={"tensor": other(k)},
+            device_id_type=pl.DeviceIdType.MESH,
+        )
+
+    def sum_arrival(k):
+        return pltpu.make_async_remote_copy(
+            src_ref=leaving.at[k],
+            dst_ref=arriving.at[other(k)],
+            send_sem=sum_send.at[k],
+            recv_sem=sum_recv.at[other(k)],
+            device_id={"tensor": other(k)},
+            device_id_type=pl.DeviceIdType.MESH,
+        )
+
+    barrier = pltpu.get_barrier_semaphore()
+    for k in range(1, devices):
+        pl.semaphore_signal(
+            barrier, inc=1, device_id={"tensor": other(k)}, device_id_type=pl.DeviceIdType.MESH
+        )
+    order = list(range(1, devices)) + [0]
+    for k in order:
+        weight_copy(k).start()
+    pl.semaphore_wait(barrier, devices - 1)
+    for k in range(1, devices):
+        att_copy(k).start()
+
+    for c in range(4):
+        cols = slice(c * I1, (c + 1) * I1)
+        for b in range(lanes // HD):
+            turned[b, cols, :] = shared_ref[b * HD : (b + 1) * HD, cols].astype(F32).T
+    sources, depth = factor_ref.shape[0], factor_ref.shape[2]
+    for h in range(heads):
+        for s in range(sources):
+            first = h * lanes + s * depth
+            factors[first : first + depth, :] = factor_ref[s, h]
+    got_att[me] = att_ref[me]
+    for k in range(1, devices):
+        att_arrival(k).wait_recv()
+
+    stack = [jnp.concatenate([got_att[t, h] for t in range(devices)], axis=0) for h in range(heads)]
+    for h in range(heads):
+        flat_att[:, h * HD : (h + 1) * HD] = stack[h]
+    stack = jnp.concatenate(stack, axis=0)
+    mask = mask_ref[...]
+    for j in range(J1):
+        table = jnp.concatenate(
+            [turned[b, pl.ds(j, HD, stride=J1), :] for b in range(lanes // HD)], axis=1
+        ).astype(BF16)
+        part = jnp.dot(stack, table, preferred_element_type=F32)
         for h in range(heads):
-            for s in range(sources):
-                first = h * lanes + s * depth
-                factors[first : first + depth, :] = factor_ref[s, h]
-        for j0 in range(0, J1, 4):
-            delta = jnp.dot(mixed[j0 * rows : (j0 + 4) * rows, :], factors[...], preferred_element_type=F32)
-            for j in range(4):
-                own = delta[j * rows : (j + 1) * rows]
-                both = jnp.concatenate([own[:, :half], own[:, half:]], axis=0)
-                spread[pl.ds(j0 + j, half, stride=J1), :] = both.T
+            own = jnp.where(mask > 0, part[h * rows : (h + 1) * rows], 0.0)
+            mixed[j * rows : (j + 1) * rows, h * lanes : (h + 1) * lanes] = own.astype(BF16)
+    for j0 in range(0, J1, 4):
+        delta = jnp.dot(mixed[j0 * rows : (j0 + 4) * rows, :], factors[...], preferred_element_type=F32)
+        for j in range(4):
+            own = delta[j * rows : (j + 1) * rows]
+            both = jnp.concatenate([own[:, :half], own[:, half:]], axis=0)
+            spread[pl.ds(j0 + j, half, stride=J1), :] = both.T
+    piece = D // 16
+    for c in range(8):
+        where = slice(c * piece, (c + 1) * piece)
+        delta_rows[:, where] = spread[where, :].T
 
     coeff = OUT_SCALE / math.sqrt(RANK * QH * HD)
-    delta = spread[pl.ds(pl.multiple_of(step * width, width), width), :].T
-    att = att_ref[...]
-    for side, weight in enumerate((low_ref, high_ref)):
-        base = jnp.dot(att, weight[...], preferred_element_type=F32)
-        out_ref[side] = (base + coeff * delta[side * rows : (side + 1) * rows]).astype(BF16)
+    per_half = D // 2 // width
+
+    def partial_of(k):
+        weight_copy(k).wait()
+        to = other(k)
+        first_row = pl.multiple_of((to // per_half) * rows, rows)
+        first_col = pl.multiple_of(lax.rem(to, per_half) * width, width)
+        base = jnp.dot(flat_att[...], weights[k], preferred_element_type=F32)
+        delta = delta_rows[pl.ds(first_row, rows), pl.ds(first_col, width)]
+        return (base + coeff * delta).astype(BF16)
+
+    def send_one(k, carry):
+        leaving[k] = partial_of(k)
+        sum_copy(k).start()
+        return carry
+
+    lax.fori_loop(1, devices, send_one, 0)
+    total = partial_of(0).astype(F32)
+    for k in range(1, devices):
+        sum_arrival(k).wait_recv()
+        total += arriving[other(k)].astype(F32)
+    out_ref[...] = total.astype(BF16)
+    for k in range(1, devices):
+        att_copy(k).wait_send()
+        sum_copy(k).wait_send()
 
 
 def project_out(attended, factors, shared, mask, w_out):
-    rows, inner = attended.shape
-    heads = inner // HD
-    lanes = mask.shape[1]
-    width = 512
-    steps = D // 2 // width
-    whole2 = lambda k: (0, 0)
-    out = pl.pallas_call(
-        functools.partial(output_kernel, heads),
-        grid=(steps,),
-        in_specs=[
-            pl.BlockSpec((rows, inner), whole2),
-            pl.BlockSpec(factors.shape, lambda k: (0, 0, 0, 0)),
-            pl.BlockSpec(shared.shape, whole2),
-            pl.BlockSpec(mask.shape, whole2),
-            pl.BlockSpec((inner, width), lambda k: (0, k)),
-            pl.BlockSpec((inner, width), lambda k: (0, k + steps)),
-        ],
-        out_specs=pl.BlockSpec((2, rows, width), lambda k: (0, 0, k)),
-        out_shape=jax.ShapeDtypeStruct((2, rows, D // 2), BF16),
+    devices, heads, rows_here, _ = attended.shape
+    rows, lanes = mask.shape
+    inner = heads * HD
+    width = D // devices
+    vmem = pl.BlockSpec(memory_space=pltpu.VMEM)
+    return pl.pallas_call(
+        functools.partial(output_kernel, devices),
+        in_specs=[vmem, vmem, vmem, vmem, pl.BlockSpec(memory_space=pl.ANY)],
+        out_specs=vmem,
+        out_shape=jax.ShapeDtypeStruct((rows, width), BF16),
         scratch_shapes=[
-            pltpu.VMEM((J1 * HD, lanes), F32),
+            pltpu.VMEM((devices, inner, width), BF16),
+            pltpu.VMEM((devices, heads, rows_here, HD), BF16),
+            pltpu.VMEM((rows, inner), BF16),
+            pltpu.VMEM((lanes // HD, J1 * HD, HD), F32),
             pltpu.VMEM((J1 * rows, heads * lanes), BF16),
             pltpu.VMEM((heads * lanes, I1), BF16),
             pltpu.VMEM((D // 2, 2 * rows), F32),
-        ],
-        compiler_params=params(),
-    )(attended, factors, shared, mask, w_out, w_out)
-    return out
+            pltpu.VMEM((2 * rows, D // 2), F32),
+            pltpu.VMEM((devices, rows, width), BF16),
+            pltpu.VMEM((devices, rows, width), BF16),
+            pltpu.SemaphoreType.DMA((devices,)),
+            pltpu.SemaphoreType.DMA((devices,)),
+            pltpu.SemaphoreType.DMA((devices,)),
+            pltpu.SemaphoreType.DMA((devices,)),
+            pltpu.SemaphoreType.DMA((devices,)),
+        ],
+        compiler_params=params(collective_id=1, has_side_effects=True),
+    )(attended, factors, shared, mask, w_out)
 
 
 def on_device(
@@ -375,28 +482,25 @@
     got_shared = lax.all_to_all(send_shared, "dp", split_axis=0, concat_axis=0, tiled=True)
     everyone = lax.all_gather(got_shared, "tensor", axis=2, tiled=True)
     tables = everyone.reshape(groups * slots, 2, RANK, J1 * HD)
-    lanes = groups * slots * RANK
-    shared_query = tables[:, 0].reshape(lanes, J1 * HD)
-    shared_out = tables[:, 1].reshape(lanes, J1 * HD)
+    lanes = groups * slots * RANK * 2
+    tables = jnp.repeat(tables, 2, axis=2).transpose(1, 0, 2, 3).reshape(2, lanes, J1 * HD)
+    shared_query, shared_out = tables[0], tables[1]
 
     picked = pick_tenants(jnp.maximum(outgoing, 0), adapter_heads)
-    picked = picked.reshape(groups, slots, heads_here, RANK, 2, I1)
-
-    def exchange(part):
-        send = picked[:, :, :, :, part, :].transpose(0, 2, 1, 3, 4)
-        send = send.reshape(groups, heads_here, slots * RANK, I1)
-        return lax.all_to_all(send, "dp", split_axis=0, concat_axis=0, tiled=True)
-
-    heads_query = exchange(0)
-    heads_out = exchange(1)
+    picked = picked.reshape(groups, slots, heads_here, RANK * 2, I1).transpose(0, 2, 1, 3, 4)
+    picked = picked.reshape(groups, heads_here, slots * RANK * 2, I1)
+    factors = lax.all_to_all(picked, "dp", split_axis=0, concat_axis=0, tiled=True)
 
     incoming = lax.dynamic_index_in_dim(tenant_lists, dp, 1, keepdims=False)
     ids = jnp.where(incoming >= 0, jnp.arange(groups, dtype=jnp.int32)[:, None] * stored + incoming, -1)
-    ids = jnp.repeat(ids.reshape(-1), RANK)
-    mask = (row_tenant[:, None] == ids[None, :]).astype(F32)
+    ids = jnp.repeat(ids.reshape(-1), RANK * 2)
+    own = row_tenant[:, None] == ids[None, :]
+    part = jnp.arange(lanes, dtype=jnp.int32)[None, :] % 2
+    mask_query = (own & (part == 0)).astype(F32)
+    mask_out = (own & (part == 1)).astype(F32)
 
     normed, base, keyval = project(hidden, norm_gain, w_query, w_keyval)
-    query = adapt_query(normed, heads_query, shared_query, mask, base)
+    query = adapt_query(normed, factors, shared_query, mask_query, base)
 
     rows_here, span, width = kv_cache.shape[1:]
     both = jnp.concatenate([query, keyval], axis=1)
@@ -408,13 +512,9 @@
     first_row = lax.axis_index("tensor") * rows_here
     lengths = lax.dynamic_slice_in_dim(cache_length, first_row, rows_here, 0)
     attended = attend(lengths, queries, fresh, kv_cache.reshape(rows_here, span, width))
-    attended = lax.all_to_all(
-        attended.reshape(rows_here, QH * HD), "tensor", split_axis=1, concat_axis=0, tiled=True
-    )
-    partial = project_out(attended, heads_out, shared_out, mask, w_out)
-    row_count = partial.shape[1]
-    partial = partial.transpose(1, 0, 2).reshape(row_count, D)
-    return lax.psum_scatter(partial, "tensor", scatter_dimension=1, tiled=True)
+    devices = QH // heads_here
+    attended = attended.reshape(rows_here, devices, heads_here, HD).transpose(1, 2, 0, 3)
+    return project_out(attended, factors, shared_out, mask_out, w_out)
 
 
 def solution(mesh):

time: 233 us -> 179 us (0.77)
  the two profiles are of different devices: /device:TPU:9 before, /device:TPU:15 now
where the time goes in v2:
time: 179 us; the launch traced here: 177 us
  Pallas kernels  91.2 us (51%)
  local copies, waits for them, and re-layouts  26.6 us (15%)
  waiting for transfers between devices  25.3 us (14%)
  between operations  13.5 us (8%)
  starting transfers between devices  9.42 us (5%)
  blocking collectives  8.03 us (4%)
  other arithmetic  2.85 us (2%)
    pallas_call x1, Pallas kernels, project_out(): pl.pallas_call(functools.partial(output_kernel, devices), in_specs=[vmem,...  37.9 us
    pallas_call x1, Pallas kernels, attend(): pl.pallas_call(functools.partial(attend_kernel, slots), in_specs=[pl.Bloc...  29.8 us
    all_gather x1, waiting for transfers between devices, on_device(): everyone = lax.all_gather(got_shared, 'tensor', axis=2, tiled=True)  16.5 us
    pallas_call x1, Pallas kernels, project(): pl.pallas_call(functools.partial(project_kernel, depth), grid=(D // depth...  12.6 us
    all_to_all x1, blocking collectives, on_device(): lax.all_to_all(send_shared, 'dp', split_axis=0, concat_axis=0, tiled=True)  8.03 us
    pallas_call x1, Pallas kernels, adapt_query(): pl.pallas_call(functools.partial(query_kernel, heads), out_shape=jax.Shap...  7.09 us
    all_to_all x1, starting transfers between devices, on_device(): lax.all_to_all(picked, 'dp', split_axis=0, concat_axis=0, tiled=True)  5.66 us
    reshape x2, local copies, waits for them, and re-layouts, on_device(): picked.reshape(groups, slots, heads_here, RANK * 2, I1)  4.38 us
  transfers between devices with their start and end apart: 4, of which 3 were waited for; matrix products, arithmetic and copies ran while one was open for 13% of the time, Pallas kernels for 9%

profile of v2, /device:TPU:15, one launch (start us, length us, event | category | flops | bytes accessed | tf_op | source)
XLA Modules:
  0.0 177.5 jit_solution(6289754673164133459)
XLA Ops:
  6.5 0.7 all-gather.3.cloned.1.call-update
  7.3 0.7 constant_dynamic-slice_fusion
  8.1 0.5 fusion
  8.6 8.0 %all_to_all.19 = bf16[4,8,4096]{2,1,0:T(8,128)(2,1)} all-to-all(bf16[4,8,4096]{2,1,0:T(8,128)(2,1)S(1)} %fusion), channel_id=1, replica_groups=mesh['groups'=2,'tensor'=4,'dp'=4] {'dp'}, dimensions={0} | all-to-all | bytes 524288 | tf_op jit(solution)/shard_map/all_to_all | solution.py:482
  16.6 0.5 broadcast_maximum_fusion.index_ref
  17.1 3.9 %shard_map.110 = bf16[32,8,4,2,512]{4,3,2,1,0:T(2,128)(2,1)} custom-call(s32[32]{0:T(128)} %broadcast_maximum_fusion.index_ref, bf16[200,8,4,2,512]{4,3,2,1,0:T(2,128)(2,1)} %store_ref.1), custom_call_target="tpu_custom_call" | custom-call | tf_op jit(solution)/shard_map/pallas_call | solution.py:43
  21.1 2.8 %reshape.77 = bf16[4,8,8,8,512]{4,3,2,1,0:T(8,128)(2,1)S(1)} reshape(bf16[32,8,4,2,512]{4,3,2,1,0:T(2,128)(2,1)} %shard_map.110) | data formatting | bytes 4194304 | tf_op jit(solution)/shard_map/reshape | solution.py:490
  23.8 1.6 copy.26
  25.5 5.7 %all-to-all-start = ((bf16[4,8,64,512]{3,2,1,0:T(8,128)(2,1)}), bf16[4,8,64,512]{3,2,1,0:T(8,128)(2,1)S(1)}, u32[]{:S(2)}, u32[]{:S(2)}) async-start(bf16[4,8,64,512]{3,2,1,0:T(8,128)(2,1)} %bitcast.24), calls=%async_computation | async-start | bytes 4194304 | tf_op jit(solution)/shard_map/all_to_all | solution.py:492
  31.1 0.7 dynamic-slice_reduce_fusion
  32.3 0.6 reshape.75.gain_ref
  32.9 0.7 fusion.2
  33.6 4.1 %all-gather.3.cloned.1.call-done.hidden_ref = bf16[64,8192]{1,0:T(8,128)(2,1)} async-done(((bf16[64,2048]{1,0:T(8,128)(2,1)}), bf16[64,8192]{1,0:T(8,128)(2,1)}) %all-gather.3.cloned.1.call-update) | async-done | bytes 1048592 | tf_op jit(solution)/shard_map/all_gather | solution.py:475
  37.7 12.6 %shard_map.109 = (bf16[64,8192]{1,0:T(8,128)(2,1)}, f32[64,1024]{1,0:T(8,128)}, bf16[64,256]{1,0:T(8,128)(2,1)}) custom-call(bf16[64,8192]{1,0:T(8,128)(2,1)} %all-gather.3.cloned.1.call-done.hidden_ref, bf16[1,8192]{1,0:T(2,128)(2,1)} %reshape.75.gain_ref, bf16[8192,1024]{1,0:T(8,128)(2,1)} %wq_ref.1, bf16[8192,256]{1,0:T(8,128)(2,1)} %wkv_ref.1), custom_call_target="tpu_custom_call" | custom-call | flops 1342177280 | bytes 20971520 | tf_op jit(solution)/shard_map/pallas_call | solution.py:81
  50.3 16.5 %all-gather.5.cloned.1.call-done = bf16[4,8,16384]{2,1,0:T(8,128)(2,1)} async-done(((bf16[4,8,4096]{2,1,0:T(8,128)(2,1)}), bf16[4,8,16384]{2,1,0:T(8,128)(2,1)}) %all-gather.5.cloned.1.call-update) | async-done | bytes 1048592 | tf_op jit(solution)/shard_map/all_gather | solution.py:483
  66.8 1.8 %reshape.80 = bf16[32,2,4,2048]{3,2,1,0:T(4,128)(2,1)S(1)} reshape(bf16[4,8,16384]{2,1,0:T(8,128)(2,1)} %all-gather.5.cloned.1.call-done) | data formatting | bytes 2097152 | tf_op jit(solution)/shard_map/reshape | solution.py:484
  68.7 0.5 copy.21
  69.1 3.5 %broadcast_in_dim.14 = bf16[32,2,4,2,2048]{4,3,2,0,1:T(2,128)(2,1)} broadcast(bf16[32,2,4,2048]{3,2,0,1:T(4,128)(2,1)S(1)} %copy.21), dimensions={0,1,2,4} | broadcast | bytes 3145728 | tf_op jit(solution)/shard_map/broadcast_in_dim | solution.py:486
  72.6 4.1 %reshape.81 = bf16[32,2,8,2048]{3,2,0,1:T(8,128)(2,1)} reshape(bf16[32,2,4,2,2048]{4,3,2,0,1:T(2,128)(2,1)} %broadcast_in_dim.14) | data formatting | bytes 4194304 | tf_op jit(solution)/shard_map/reshape | solution.py:486
  76.7 3.2 %slice_bitcast_fusion = (bf16[256,2048]{1,0:T(8,128)(2,1)}, bf16[256,2048]{1,0:T(8,128)(2,1)}) fusion(bf16[2,32,8,2048]{3,2,1,0:T(8,128)(2,1)} %bitcast.25), kind=kLoop, calls=%fused_computation.3 | loop fusion | bytes 4194304 | tf_op jit(solution)/shard_map/squeeze | solution.py:487
  79.9 1.3 copy-done.2
  81.2 7.1 %shard_map.111 = bf16[64,1024]{1,0:T(8,128)(2,1)} custom-call(bf16[64,8192]{1,0:T(8,128)(2,1)} %get-tuple-element.8.normed_ref, bf16[4,8,64,512]{3,2,1,0:T(8,128)(2,1)} %copy-done.2, bf16[256,2048]{1,0:T(8,128)(2,1)} %get-tuple-element.12.shared_ref, f32[64,256]{1,0:T(8,128)} %get-tuple-element.14.mask_ref, f32[64,1024]{1,0:T(8,128)} %get-tuple-element.9.base_ref), custom_call_target="tpu_custom_call" | custom-call | tf_op jit(solution)/shard_map/pallas_call | solution.py:145
  88.3 1.6 pad_maximum_fusion
  89.9 3.7 %all-to-all-start.2 = ((bf16[4,16,1280]{2,1,0:T(8,128)(2,1)}), bf16[4,16,1280]{2,1,0:T(8,128)(2,1)S(1)}, u32[]{:S(2)}, u32[]{:S(2)}) async-start(bf16[4,16,1280]{2,1,0:T(8,128)(2,1)} %bitcast.5), calls=%async_computation.2 | async-start | bytes 327680 | tf_op jit(solution)/shard_map/all_to_all | solution.py:507
  93.6 0.6 dynamic_slice.11.length_ref
  94.2 4.0 %all-to-all-done.2 = bf16[4,16,1280]{2,1,0:T(8,128)(2,1)S(1)} async-done(((bf16[4,16,1280]{2,1,0:T(8,128)(2,1)}), bf16[4,16,1280]{2,1,0:T(8,128)(2,1)S(1)}, u32[]{:S(2)}, u32[]{:S(2)}) %all-to-all-start.2) | async-done | bytes 163872 | tf_op jit(solution)/shard_map/all_to_all | solution.py:507
  98.3 0.7 reshape.82.query_ref
  99.0 0.6 reshape.83.fresh_ref
  99.7 29.8 %shard_map.112 = bf16[16,32,128]{2,1,0:T(8,128)(2,1)} custom-call(s32[16]{0:T(128)} %dynamic_slice.11.length_ref, bf16[16,32,128]{2,1,0:T(8,128)(2,1)} %reshape.82.query_ref, bf16[16,8,128]{2,1,0:T(8,128)(2,1)} %reshape.83.fresh_ref, bf16[16,2048,1024]{2,1,0:T(8,128)(2,1)} %bitcast.8.cache_ref), custom_call_target="tpu_custom_call" | custom-call | flops 536870912 | bytes 33554432 | tf_op jit(solution)/shard_map/pallas_call | solution.py:247
  129.4 1.6 copy.24
  131.1 37.9 %shard_map.113 = bf16[64,2048]{1,0:T(8,128)(2,1)} custom-call(bf16[4,8,16,128]{3,2,1,0:T(8,128)(2,1)} %bitcast.26, bf16[4,8,64,512]{3,2,1,0:T(8,128)(2,1)} %copy-done.2, bf16[256,2048]{1,0:T(8,128)(2,1)} %get-tuple-element.11.shared_ref, f32[64,256]{1,0:T(8,128)} %get-tuple-element.13.mask_ref, bf16[1024,8192]{1,0:T(8,128)(2,1)} %weight_ref.1), custom_call_target="tpu_custom_call" | custom-call | tf_op jit(solution)/shard_map/pallas_call | solution.py:431
  168.9 1.7 copy.28
  (30 shorter events, 0.7 us)
Async XLA Ops:
  6.5 1.5 copy-start
  6.5 31.2 %all-gather.3.cloned.1.call-start = ((), (), s32[]{:S(2)}) async-start(), calls=%async_computation.3 | async-start | bytes 1310720 | tf_op jit(solution)/shard_map/all_gather | solution.py:475
  7.3 59.6 %all-gather.5.cloned.1.call-start = ((), (), s32[]{:S(2)}) async-start(), calls=%async_computation.4 | async-start | bytes 1310720 | tf_op jit(solution)/shard_map/all_gather | solution.py:483
  25.5 6.8 %copy-start.4 = (bf16[8192]{0:T(1024)(128)(2,1)S(1)}, bf16[8192]{0:T(1024)(128)(2,1)}, u32[]{:S(2)}) copy-start(bf16[8192]{0:T(1024)(128)(2,1)} %param.12) | copy-start | bytes 49156
  25.5 7.5 %copy-start.5 = (s32[64]{0:T(128)S(1)}, s32[64]{0:T(128)}, u32[]{:S(2)}) copy-start(s32[64]{0:T(128)} %param.18) | copy-start | bytes 772
  25.5 54.4 %all-to-all-start = ((bf16[4,8,64,512]{3,2,1,0:T(8,128)(2,1)}), bf16[4,8,64,512]{3,2,1,0:T(8,128)(2,1)S(1)}, u32[]{:S(2)}, u32[]{:S(2)}) async-start(bf16[4,8,64,512]{3,2,1,0:T(8,128)(2,1)} %bitcast.24), calls=%async_computation | async-start | bytes 4194304 | tf_op jit(solution)/shard_map/all_to_all | solution.py:492
  79.9 1.3 copy-start.2
  81.2 7.1 %copy-start.3 = (bf16[64,256]{1,0:T(8,128)(2,1)S(1)}, bf16[64,256]{1,0:T(8,128)(2,1)}, u32[]{:S(2)}) copy-start(bf16[64,256]{1,0:T(8,128)(2,1)} %get-tuple-element.10) | copy-start | bytes 98308
  81.2 12.4 %copy-start.6 = (s32[64]{0:T(128)S(1)}, s32[64]{0:T(128)}, u32[]{:S(2)}) copy-start(s32[64]{0:T(128)} %param.17) | copy-start | bytes 772
  89.9 8.3 %all-to-all-start.2 = ((bf16[4,16,1280]{2,1,0:T(8,128)(2,1)}), bf16[4,16,1280]{2,1,0:T(8,128)(2,1)S(1)}, u32[]{:S(2)}, u32[]{:S(2)}) async-start(bf16[4,16,1280]{2,1,0:T(8,128)(2,1)} %bitcast.5), calls=%async_computation.2 | async-start | bytes 327680 | tf_op jit(solution)/shard_map/all_to_all | solution.py:507
  131.1 39.6 %copy-start.1 = (bf16[200,4096]{1,0:T(8,128)(2,1)S(1)}, bf16[200,4096]{1,0:T(8,128)(2,1)}, u32[]{:S(2)}) copy-start(bf16[200,4096]{1,0:T(8,128)(2,1)} %param.21) | copy-start | bytes 4915204
Sparse Core Ops, SparseCore 0:
  8.9 28.7 all-gather.2
  39.3 27.4 all-gather.4

commit v3 on v2

--- a/solution.py
+++ b/solution.py
@@ -53,68 +53,157 @@
     )(indices, store)
 
 
-def project_kernel(depth, hidden_ref, gain_ref, wq_ref, wkv_ref, normed_ref, base_ref, keyval_ref, acc):
-    step = pl.program_id(0)
-
-    @pl.when(step == 0)
-    def _():
-        wide = hidden_ref[...].astype(F32)
-        inverse = lax.rsqrt(jnp.mean(wide * wide, axis=1, keepdims=True) + 1e-05)
-        normed_ref[...] = (wide * inverse * gain_ref[...].astype(F32)).astype(BF16)
-        base_ref[...] = jnp.zeros_like(base_ref)
-        acc[...] = jnp.zeros_like(acc)
-
-    part = normed_ref[:, pl.ds(pl.multiple_of(step * depth, depth), depth)]
-    base_ref[...] += jnp.dot(part, wq_ref[...], preferred_element_type=F32)
-    acc[...] += jnp.dot(part, wkv_ref[...], preferred_element_type=F32)
-
-    @pl.when(step == pl.num_programs(0) - 1)
-    def _():
-        keyval_ref[...] = acc[...].astype(BF16)
-
-
-def project(hidden, gain, w_query, w_keyval):
-    rows = hidden.shape[0]
-    depth = 1024
-    q_cols, kv_cols = w_query.shape[1], w_keyval.shape[1]
-    whole = lambda k: (0, 0)
-    return pl.pallas_call(
-        functools.partial(project_kernel, depth),
-        grid=(D // depth,),
-        in_specs=[
-            pl.BlockSpec((rows, D), whole),
-            pl.BlockSpec((1, D), whole),
-            pl.BlockSpec((depth, q_cols), lambda k: (k, 0)),
-            pl.BlockSpec((depth, kv_cols), lambda k: (k, 0)),
-        ],
-        out_specs=[
-            pl.BlockSpec((rows, D), whole),
-            pl.BlockSpec((rows, q_cols), whole),
-            pl.BlockSpec((rows, kv_cols), whole),
-        ],
-        out_shape=[
-            jax.ShapeDtypeStruct((rows, D), BF16),
-            jax.ShapeDtypeStruct((rows, q_cols), F32),
-            jax.ShapeDtypeStruct((rows, kv_cols), BF16),
-        ],
-        scratch_shapes=[pltpu.VMEM((rows, kv_cols), F32)],
-        compiler_params=params(),
-        cost_estimate=pl.CostEstimate(
-            flops=2 * rows * D * (q_cols + kv_cols),
-            bytes_accessed=2 * D * (q_cols + kv_cols),
-            transcendentals=0,
-        ),
-    )(hidden, gain.reshape(1, D), w_query, w_keyval)
-
-
-def query_kernel(heads, normed_ref, factor_ref, shared_ref, mask_ref, base_ref, query_ref, turned, spread, inner):
-    rows = normed_ref.shape[0]
-    lanes = mask_ref.shape[1]
+def mesh_copy(source, target, send_sem, recv_sem, axis, place):
+    return pltpu.make_async_remote_copy(
+        src_ref=source,
+        dst_ref=target,
+        send_sem=send_sem,
+        recv_sem=recv_sem,
+        device_id={axis: place},
+        device_id_type=pl.DeviceIdType.MESH,
+    )
+
+
+def expand_shared(blocks, first, lanes, store):
+    tenants, width = blocks.shape[1], blocks.shape[2]
+    span = J1 * HD
+    piece = min(width, span)
+    lane = lax.broadcasted_iota(jnp.int32, (lanes, RANK * tenants), 0)
+    entry = lax.broadcasted_iota(jnp.int32, (lanes, RANK * tenants), 1)
+    wanted = (lane // 2) % RANK * tenants + lane // (2 * RANK)
+    chooser = (wanted == entry).astype(F32).astype(BF16)
+    for col in range(0, span, piece):
+        stack = []
+        for r in range(RANK):
+            start = first + r * span + col
+            local = start % width
+            stack.append(blocks[start // width, :, local : local + piece])
+        stack = jnp.concatenate(stack, axis=0)
+        store(col, piece, jnp.dot(chooser, stack, preferred_element_type=F32))
+
+
+def front_kernel(
+    devices,
+    groups,
+    hidden_ref,
+    gain_ref,
+    factor_ref,
+    shared_ref,
+    mask_ref,
+    wq_ref,
+    wkv_ref,
+    factors_out,
+    shared_out,
+    rows_out,
+    wq,
+    wkv,
+    hidden,
+    factors,
+    first_hop,
+    blocks,
+    normed,
+    turned,
+    spread,
+    inner,
+    table,
+    leaving,
+    arriving,
+    weight_sems,
+    hidden_send,
+    hidden_recv,
+    factor_send,
+    factor_recv,
+    hop_send,
+    hop_recv,
+    block_send,
+    block_recv,
+    row_send,
+    row_recv,
+):
+    me, dp = lax.axis_index("tensor"), lax.axis_index("dp")
+    rows, lanes = mask_ref.shape
+    heads = factor_ref.shape[1]
+    width = hidden_ref.shape[1]
+    chunks, depth = wq.shape[0], wq.shape[1]
+    rows_here = arriving.shape[1]
+    q_cols = wq.shape[2]
+
+    def peer(k):
+        return lax.rem(me + k, devices)
+
+    def mate(k):
+        return lax.rem(dp + k, groups)
+
+    def weight_copies(c):
+        where = pl.ds(c * depth, depth)
+        return (
+            pltpu.make_async_copy(wq_ref.at[where], wq.at[c], weight_sems.at[0, c]),
+            pltpu.make_async_copy(wkv_ref.at[where], wkv.at[c], weight_sems.at[1, c]),
+        )
+
+    def hidden_copy(k, to):
+        return mesh_copy(hidden_ref, hidden.at[to], hidden_send.at[k], hidden_recv.at[to], "tensor", peer(k))
+
+    def block_copy(k, to):
+        return mesh_copy(blocks.at[me], blocks.at[to], block_send.at[k], block_recv.at[to], "tensor", peer(k))
+
+    def row_copy(k, to):
+        return mesh_copy(leaving.at[peer(k)], arriving.at[to], row_send.at[k], row_recv.at[to], "tensor", peer(k))
+
+    def hop_copy(k, to):
+        return mesh_copy(shared_ref.at[mate(k)], first_hop.at[to], hop_send.at[k], hop_recv.at[to], "dp", mate(k))
+
+    def factor_copy(k, to):
+        return mesh_copy(factor_ref.at[mate(k)], factors.at[to], factor_send.at[k], factor_recv.at[to], "dp", mate(k))
+
+    barrier = pltpu.get_barrier_semaphore()
+    for k in range(1, devices):
+        pl.semaphore_signal(barrier, inc=1, device_id={"tensor": peer(k)}, device_id_type=pl.DeviceIdType.MESH)
+    for k in range(1, groups):
+        pl.semaphore_signal(barrier, inc=1, device_id={"dp": mate(k)}, device_id_type=pl.DeviceIdType.MESH)
+    for c in range(chunks):
+        for copy in weight_copies(c):
+            copy.start()
+    pl.semaphore_wait(barrier, devices - 1 + groups - 1)
+    for k in range(1, groups):
+        hop_copy(k, dp).start()
+    for k in range(1, devices):
+        hidden_copy(k, me).start()
+    for k in range(1, groups):
+        factor_copy(k, dp).start()
+    first_hop[dp] = shared_ref[dp]
+    hidden[me] = hidden_ref[...]
+    factors[dp] = factor_ref[dp]
+    for k in range(1, groups):
+        hop_copy(k, mate(k)).wait_recv()
+    blocks[me] = jnp.concatenate([first_hop[s].astype(F32) for s in range(groups)], axis=0).astype(BF16)
+    for k in range(1, devices):
+        block_copy(k, me).start()
+
+    for k in range(1, devices):
+        hidden_copy(k, peer(k)).wait_recv()
+    squares = jnp.zeros((rows, 1), F32)
+    for t in range(devices):
+        wide = hidden[t].astype(F32)
+        squares += jnp.sum(wide * wide, axis=1, keepdims=True)
+    inverse = lax.rsqrt(squares / D + 1e-05)
+    for t in range(devices):
+        where = slice(t * width, (t + 1) * width)
+        normed[:, where] = (hidden[t].astype(F32) * inverse * gain_ref[:, where].astype(F32)).astype(BF16)
+    base = jnp.zeros((rows, q_cols), F32)
+    keyval = jnp.zeros((rows, wkv.shape[2]), F32)
+    for c in range(chunks):
+        for copy in weight_copies(c):
+            copy.wait()
+        part = normed[:, c * depth : (c + 1) * depth]
+        base += jnp.dot(part, wq[c], preferred_element_type=F32)
+        keyval += jnp.dot(part, wkv[c], preferred_element_type=F32)
+
     half = D // 2
     piece = half // 4
     for c in range(4):
         both = jnp.concatenate(
-            [normed_ref[:, c * piece : (c + 1) * piece], normed_ref[:, half + c * piece : half + (c + 1) * piece]],
+            [normed[:, c * piece : (c + 1) * piece], normed[:, half + c * piece : half + (c + 1) * piece]],
             axis=0,
         ).astype(F32)
         turned[c * piece : (c + 1) * piece, :] = both.T
@@ -122,36 +211,99 @@
         back = turned[pl.ds(j, I1 // 2, stride=J1), :].T
         spread[j * rows : (j + 1) * rows, : I1 // 2] = back[:rows].astype(BF16)
         spread[j * rows : (j + 1) * rows, I1 // 2 :] = back[rows:].astype(BF16)
+
+    for k in range(1, groups):
+        factor_copy(k, mate(k)).wait_recv()
     mask = mask_ref[...]
     for h in range(heads):
-        factor = jnp.concatenate([factor_ref[s, h] for s in range(factor_ref.shape[0])], axis=0)
+        factor = jnp.concatenate([factors[s, h] for s in range(groups)], axis=0)
         for j0 in range(0, J1, 4):
             part = nt_dot(spread[j0 * rows : (j0 + 4) * rows, :], factor)
             for j in range(4):
                 own = jnp.where(mask > 0, part[j * rows : (j + 1) * rows], 0.0)
                 inner[j0 + j, h * rows : (h + 1) * rows, :] = own.astype(BF16)
+    factors_out[...] = factors[...]
+
+    for k in range(1, devices):
+        block_copy(k, peer(k)).wait_recv()
+
+    def store(col, size, value):
+        table[:, col : col + size] = value.astype(BF16)
+
+    expand_shared(blocks, 0, lanes, store)
+    shared_out[...] = blocks[...]
     delta = jnp.zeros((heads * rows, HD), F32)
     for j in range(J1):
-        delta += jnp.dot(inner[j], shared_ref[:, j * HD : (j + 1) * HD], preferred_element_type=F32)
+        delta += jnp.dot(inner[j], table[:, j * HD : (j + 1) * HD], preferred_element_type=F32)
     coeff = 1.0 / math.sqrt(RANK * D)
-    for h in range(heads):
-        cols = slice(h * HD, (h + 1) * HD)
-        query_ref[:, cols] = (base_ref[:, cols] + coeff * delta[h * rows : (h + 1) * rows]).astype(BF16)
-
-
-def adapt_query(normed, factors, shared, mask, base):
-    rows, cols = base.shape
-    heads = cols // HD
+    query = jnp.concatenate(
+        [base[:, h * HD : (h + 1) * HD] + coeff * delta[h * rows : (h + 1) * rows] for h in range(heads)], axis=1
+    )
+    for t in range(devices):
+        where = slice(t * rows_here, (t + 1) * rows_here)
+        leaving[t, :, :q_cols] = query[where].astype(BF16)
+        leaving[t, :, q_cols:] = keyval[where].astype(BF16)
+    for k in range(1, devices):
+        row_copy(k, me).start()
+    arriving[me] = leaving[me]
+    for k in range(1, devices):
+        row_copy(k, peer(k)).wait_recv()
+    rows_out[...] = arriving[...]
+    for k in range(1, devices):
+        hidden_copy(k, me).wait_send()
+        block_copy(k, me).wait_send()
+        row_copy(k, me).wait_send()
+    for k in range(1, groups):
+        hop_copy(k, dp).wait_send()
+        factor_copy(k, dp).wait_send()
+
+
+def front(hidden, gain, factors, shared, mask, w_query, w_keyval, devices):
+    rows, lanes = mask.shape
+    groups, heads = factors.shape[:2]
+    slots, width = shared.shape[1:]
+    q_cols, kv_cols = w_query.shape[1], w_keyval.shape[1]
+    cols = q_cols + kv_cols
+    chunks = 8
+    vmem = pl.BlockSpec(memory_space=pltpu.VMEM)
+    anywhere = pl.BlockSpec(memory_space=pl.ANY)
     return pl.pallas_call(
-        functools.partial(query_kernel, heads),
-        out_shape=jax.ShapeDtypeStruct((rows, cols), BF16),
+        functools.partial(front_kernel, devices, groups),
+        in_specs=[vmem, vmem, vmem, vmem, vmem, anywhere, anywhere],
+        out_specs=[vmem, vmem, vmem],
+        out_shape=[
+            jax.ShapeDtypeStruct(factors.shape, BF16),
+            jax.ShapeDtypeStruct((devices, groups * slots, width), BF16),
+            jax.ShapeDtypeStruct((devices, rows // devices, cols), BF16),
+        ],
         scratch_shapes=[
+            pltpu.VMEM((chunks, D // chunks, q_cols), BF16),
+            pltpu.VMEM((chunks, D // chunks, kv_cols), BF16),
+            pltpu.VMEM((devices,) + hidden.shape, BF16),
+            pltpu.VMEM(factors.shape, BF16),
+            pltpu.VMEM((groups, slots, width), BF16),
+            pltpu.VMEM((devices, groups * slots, width), BF16),
+            pltpu.VMEM((rows, D), BF16),
             pltpu.VMEM((D // 2, 2 * rows), F32),
             pltpu.VMEM((J1 * rows, I1), BF16),
-            pltpu.VMEM((J1, heads * rows, mask.shape[1]), BF16),
+            pltpu.VMEM((J1, heads * rows, lanes), BF16),
+            pltpu.VMEM((lanes, J1 * HD), BF16),
+            pltpu.VMEM((devices, rows // devices, cols), BF16),
+            pltpu.VMEM((devices, rows // devices, cols), BF16),
+            pltpu.SemaphoreType.DMA((2, chunks)),
+            pltpu.SemaphoreType.DMA((devices,)),
+            pltpu.SemaphoreType.DMA((devices,)),
+            pltpu.SemaphoreType.DMA((groups,)),
+            pltpu.SemaphoreType.DMA((groups,)),
+            pltpu.SemaphoreType.DMA((groups,)),
+            pltpu.SemaphoreType.DMA((groups,)),
+            pltpu.SemaphoreType.DMA((devices,)),
+            pltpu.SemaphoreType.DMA((devices,)),
+            pltpu.SemaphoreType.DMA((devices,)),
+            pltpu.SemaphoreType.DMA((devices,)),
         ],
-        compiler_params=params(),
-    )(normed, factors, shared, mask, base)
+        compiler_params=params(collective_id=2, has_side_effects=True),
+    )(hidden, gain.reshape(1, D), factors, shared, mask, w_query, w_keyval)
 
 
 def attend_kernel(slots, length_ref, query_ref, fresh_ref, cache_ref, out_ref, held, scores, sems):
@@ -357,10 +509,11 @@
     for k in range(1, devices):
         att_copy(k).start()
 
-    for c in range(4):
-        cols = slice(c * I1, (c + 1) * I1)
+    def store(col, size, value):
         for b in range(lanes // HD):
-            turned[b, cols, :] = shared_ref[b * HD : (b + 1) * HD, cols].astype(F32).T
+            turned[b, col : col + size, :] = value[b * HD : (b + 1) * HD].T
+
+    expand_shared(shared_ref, RANK * J1 * HD, lanes, store)
     sources, depth = factor_ref.shape[0], factor_ref.shape[2]
     for h in range(heads):
         for s in range(sources):
@@ -472,24 +625,16 @@
     dp = lax.axis_index("dp")
     outgoing = lax.dynamic_index_in_dim(tenant_lists, dp, 0, keepdims=False).reshape(-1)
 
-    hidden = lax.all_gather(hidden_in, "tensor", axis=1, tiled=True)
     picker = (outgoing[:, None] == jnp.arange(stored, dtype=jnp.int32)[None, :]).astype(BF16)
     send_shared = (
         jnp.dot(picker, adapter_shared, preferred_element_type=F32)
         .astype(BF16)
         .reshape(groups, slots, adapter_shared.shape[1])
     )
-    got_shared = lax.all_to_all(send_shared, "dp", split_axis=0, concat_axis=0, tiled=True)
-    everyone = lax.all_gather(got_shared, "tensor", axis=2, tiled=True)
-    tables = everyone.reshape(groups * slots, 2, RANK, J1 * HD)
     lanes = groups * slots * RANK * 2
-    tables = jnp.repeat(tables, 2, axis=2).transpose(1, 0, 2, 3).reshape(2, lanes, J1 * HD)
-    shared_query, shared_out = tables[0], tables[1]
-
     picked = pick_tenants(jnp.maximum(outgoing, 0), adapter_heads)
     picked = picked.reshape(groups, slots, heads_here, RANK * 2, I1).transpose(0, 2, 1, 3, 4)
     picked = picked.reshape(groups, heads_here, slots * RANK * 2, I1)
-    factors = lax.all_to_all(picked, "dp", split_axis=0, concat_axis=0, tiled=True)
 
     incoming = lax.dynamic_index_in_dim(tenant_lists, dp, 1, keepdims=False)
     ids = jnp.where(incoming >= 0, jnp.arange(groups, dtype=jnp.int32)[:, None] * stored + incoming, -1)
@@ -499,22 +644,19 @@
     mask_query = (own & (part == 0)).astype(F32)
     mask_out = (own & (part == 1)).astype(F32)
 
-    normed, base, keyval = project(hidden, norm_gain, w_query, w_keyval)
-    query = adapt_query(normed, factors, shared_query, mask_query, base)
-
+    devices = QH // heads_here
+    factors, shared, parts = front(
+        hidden_in, norm_gain, picked, send_shared, mask_query, w_query, w_keyval, devices
+    )
     rows_here, span, width = kv_cache.shape[1:]
-    both = jnp.concatenate([query, keyval], axis=1)
-    both = lax.all_to_all(both, "tensor", split_axis=0, concat_axis=0, tiled=True)
-    parts = both.reshape(-1, rows_here, both.shape[1])
-    q_cols = query.shape[1]
+    q_cols = heads_here * HD
     queries = parts[:, :, :q_cols].transpose(1, 0, 2).reshape(rows_here, QH, HD)
     fresh = parts[:, :, q_cols:].transpose(1, 0, 2).reshape(rows_here, 2 * KVH, HD)
     first_row = lax.axis_index("tensor") * rows_here
     lengths = lax.dynamic_slice_in_dim(cache_length, first_row, rows_here, 0)
     attended = attend(lengths, queries, fresh, kv_cache.reshape(rows_here, span, width))
-    devices = QH // heads_here
     attended = attended.reshape(rows_here, devices, heads_here, HD).transpose(1, 2, 0, 3)
-    return project_out(attended, factors, shared_out, mask_out, w_out)
+    return project_out(attended, factors, shared, mask_out, w_out)
 
 
 def solution(mesh):

time: 179 us -> 152 us (0.85)
  the two profiles are of different devices: /device:TPU:15 before, /device:TPU:9 now
where the time goes in v3:
time: 152 us; the launch traced here: 151 us
  Pallas kernels  129 us (85%)
  local copies, waits for them, and re-layouts  18.4 us (12%)
  other arithmetic  1.89 us (1%)
    pallas_call x1, Pallas kernels, front(): pl.pallas_call(functools.partial(front_kernel, devices, groups), in_specs...  58.2 us
    pallas_call x1, Pallas kernels, project_out(): pl.pallas_call(functools.partial(output_kernel, devices), in_specs=[vmem,...  37.7 us
    pallas_call x1, Pallas kernels, attend(): pl.pallas_call(functools.partial(attend_kernel, slots), in_specs=[pl.Bloc...  28.6 us
    reshape x2, local copies, waits for them, and re-layouts, on_device(): picked.reshape(groups, slots, heads_here, RANK * 2, I1)  7.3 us
    pallas_call x1, Pallas kernels, pick_tenants(): pl.pallas_call(functools.partial(pick_kernel, count), in_specs=[pl.BlockS...  4.52 us

profile of v3, /device:TPU:9, one launch (start us, length us, event | category | flops | bytes accessed | tf_op | source)
XLA Modules:
  0.0 150.5 jit_solution(10682076443348086566)
XLA Ops:
  0.0 0.0 copy-start
  0.0 1.4 dynamic_slice.11.length_ref
  1.4 0.1 add.38
  1.5 0.1 add.39
  1.6 0.7 dynamic-slice_reduce_fusion
  2.3 0.1 squeeze.6
  2.4 0.7 constant_dynamic-slice_fusion
  3.1 0.1 reshape.61
  3.2 0.5 compare_select_fusion
  3.7 0.1 broadcast_in_dim.12
  3.7 0.1 eq.52
  3.8 1.3 reshape.60.gain_ref
  5.2 1.4 fusion.2
  6.6 0.0 copy-done
  6.6 1.2 fusion.shared_ref
  7.7 4.5 %shard_map.109 = bf16[32,8,4,2,512]{4,3,2,1,0:T(2,128)(2,1)} custom-call(s32[32]{0:T(128)} %get-tuple-element.14.index_ref, bf16[200,8,4,2,512]{4,3,2,1,0:T(2,128)(2,1)} %store_ref.1), custom_call_target="tpu_custom_call" | custom-call | tf_op jit(solution)/shard_map/pallas_call | solution.py:43
  12.3 4.1 %reshape.62 = bf16[4,8,8,8,512]{4,3,2,1,0:T(8,128)(2,1)} reshape(bf16[32,8,4,2,512]{4,3,2,1,0:T(2,128)(2,1)} %shard_map.109) | data formatting | bytes 4194304 | tf_op jit(solution)/shard_map/reshape | solution.py:636
  16.4 3.2 %copy.21 = bf16[4,8,8,8,512]{4,3,1,2,0:T(8,128)(2,1)} copy(bf16[4,8,8,8,512]{4,3,2,1,0:T(8,128)(2,1)} %reshape.62) | data formatting | bytes 4194304 | tf_op jit(solution)/shard_map/reshape | solution.py:636
  19.6 58.2 %shard_map.110 = (bf16[4,8,64,512]{3,2,1,0:T(8,128)(2,1)}, bf16[4,32,4096]{2,1,0:T(8,128)(2,1)}, bf16[4,16,1280]{2,1,0:T(8,128)(2,1)}) custom-call(bf16[64,2048]{1,0:T(8,128)(2,1)} %hidden_ref.1, bf16[1,8192]{1,0:T(2,128)(2,1)} %reshape.60.gain_ref, bf16[4,8,64,512]{3,2,1,0:T(8,128)(2,1)} %bitcast.16, bf16[4,8,4096]{2,1,0:T(8,128)(2,1)} %fusion.shared_ref, ...), custom_call_target="tpu_custom_call" | custom-call | tf_op jit(solution)/shard_map/pallas_call | solution.py:270
  77.8 0.8 slice_bitcast_fusion.1
  78.5 0.9 slice_bitcast_fusion
  79.4 0.1 copy.17
  79.6 0.7 reshape.65.query_ref
  80.3 0.6 reshape.66.fresh_ref
  80.9 28.6 %shard_map.111 = bf16[16,32,128]{2,1,0:T(8,128)(2,1)} custom-call(s32[16]{0:T(128)} %dynamic_slice.11.length_ref, bf16[16,32,128]{2,1,0:T(8,128)(2,1)} %reshape.65.query_ref, bf16[16,8,128]{2,1,0:T(8,128)(2,1)} %reshape.66.fresh_ref, bf16[16,2048,1024]{2,1,0:T(8,128)(2,1)} %bitcast.5.cache_ref), custom_call_target="tpu_custom_call" | custom-call | flops 536870912 | bytes 33554432 | tf_op jit(solution)/shard_map/pallas_call | solution.py:399
  109.5 1.6 %copy.19 = bf16[16,32,128]{2,0,1:T(8,128)(2,1)} copy(bf16[16,32,128]{2,1,0:T(8,128)(2,1)} %shard_map.111) | data formatting | bytes 262144 | tf_op jit(solution)/shard_map/pallas_call | solution.py:399
  111.1 37.7 %shard_map.112 = bf16[64,2048]{1,0:T(8,128)(2,1)} custom-call(bf16[4,8,16,128]{3,2,1,0:T(8,128)(2,1)} %bitcast.17, bf16[4,8,64,512]{3,2,1,0:T(8,128)(2,1)} %get-tuple-element.9.factor_ref, bf16[4,32,4096]{2,1,0:T(8,128)(2,1)} %get-tuple-element.10.shared_ref, f32[64,256]{1,0:T(8,128)} %get-tuple-element.11.mask_ref, bf16[1024,8192]{1,0:T(8,128)(2,1)} %weight_ref.1), custom_call_target="tpu_custom_call" | custom-call | tf_op jit(solution)/shard_map/pallas_call | solution.py:584
  148.9 1.7 %copy.23 = bf16[64,2048]{1,0:T(8,128)(2,1)} copy(bf16[64,2048]{1,0:T(8,128)(2,1)} %shard_map.112) | data formatting | bytes 524288
  (3 shorter events, 0.0 us)
Async XLA Ops:
  0.0 6.6 %copy-start = (bf16[200,4096]{1,0:T(8,128)(2,1)S(1)}, bf16[200,4096]{1,0:T(8,128)(2,1)}, u32[]{:S(2)}) copy-start(bf16[200,4096]{1,0:T(8,128)(2,1)} %param.21) | copy-start | bytes 4915204

commit v4 on v3

--- a/solution.py
+++ b/solution.py
@@ -62,6 +62,48 @@
         device_id={axis: place},
         device_id_type=pl.DeviceIdType.MESH,
     )
+
+
+def stack_factors(factors, head):
+    sources, slots = factors.shape[:2]
+    pieces = [factors[s, k, head].astype(F32) for s in range(sources) for k in range(slots)]
+    return jnp.concatenate(pieces, axis=0).astype(BF16)
+
+
+class Line:
+    def __init__(self, devices, me, buffer, send, recv):
+        self.devices, self.me, self.buffer, self.send, self.recv = devices, me, buffer, send, recv
+
+    def copy(self, source, side, hop):
+        step = 1 if side == 0 else -1
+        place = lax.rem(self.me + step + self.devices, self.devices)
+        block = self.buffer.at[source]
+        return mesh_copy(block, block, self.send.at[side, hop], self.recv.at[source], "tensor", place)
+
+    def legs(self, hop):
+        for side in range(2):
+            source = self.me - hop if side == 0 else self.me + hop
+            there = source >= 0 if side == 0 else source < self.devices
+            more = self.me + 1 < self.devices if side == 0 else self.me >= 1
+            yield side, source, there, there & more
+
+    def move(self, hop):
+        for side, source, there, onward in self.legs(hop):
+            if hop:
+                @pl.when(there)
+                def _(side=side, source=source):
+                    self.copy(source, side, hop).wait_recv()
+
+            @pl.when(onward)
+            def _(side=side, source=source):
+                self.copy(source, side, hop).start()
+
+    def finish(self):
+        for hop in range(self.devices - 1):
+            for side, source, _, onward in self.legs(hop):
+                @pl.when(onward)
+                def _(side=side, source=source, hop=hop):
+                    self.copy(source, side, hop).wait_send()
 
 
 def expand_shared(blocks, first, lanes, store):
@@ -122,7 +164,7 @@
 ):
     me, dp = lax.axis_index("tensor"), lax.axis_index("dp")
     rows, lanes = mask_ref.shape
-    heads = factor_ref.shape[1]
+    heads = factor_ref.shape[2]
     width = hidden_ref.shape[1]
     chunks, depth = wq.shape[0], wq.shape[1]
     rows_here = arriving.shape[1]
@@ -141,11 +183,8 @@
             pltpu.make_async_copy(wkv_ref.at[where], wkv.at[c], weight_sems.at[1, c]),
         )
 
-    def hidden_copy(k, to):
-        return mesh_copy(hidden_ref, hidden.at[to], hidden_send.at[k], hidden_recv.at[to], "tensor", peer(k))
-
-    def block_copy(k, to):
-        return mesh_copy(blocks.at[me], blocks.at[to], block_send.at[k], block_recv.at[to], "tensor", peer(k))
+    features = Line(devices, me, hidden, hidden_send, hidden_recv)
+    shares = Line(devices, me, blocks, block_send, block_recv)
 
     def row_copy(k, to):
         return mesh_copy(leaving.at[peer(k)], arriving.at[to], row_send.at[k], row_recv.at[to], "tensor", peer(k))
@@ -167,21 +206,19 @@
     pl.semaphore_wait(barrier, devices - 1 + groups - 1)
     for k in range(1, groups):
         hop_copy(k, dp).start()
-    for k in range(1, devices):
-        hidden_copy(k, me).start()
+    hidden[me] = hidden_ref[...]
+    features.move(0)
     for k in range(1, groups):
         factor_copy(k, dp).start()
     first_hop[dp] = shared_ref[dp]
-    hidden[me] = hidden_ref[...]
     factors[dp] = factor_ref[dp]
     for k in range(1, groups):
         hop_copy(k, mate(k)).wait_recv()
     blocks[me] = jnp.concatenate([first_hop[s].astype(F32) for s in range(groups)], axis=0).astype(BF16)
-    for k in range(1, devices):
-        block_copy(k, me).start()
-
-    for k in range(1, devices):
-        hidden_copy(k, peer(k)).wait_recv()
+    for hop in range(1, devices):
+        features.move(hop)
+        if hop == 1:
+            shares.move(0)
     squares = jnp.zeros((rows, 1), F32)
     for t in range(devices):
         wide = hidden[t].astype(F32)
@@ -199,6 +236,7 @@
         base += jnp.dot(part, wq[c], preferred_element_type=F32)
         keyval += jnp.dot(part, wkv[c], preferred_element_type=F32)
 
+    shares.move(1)
     half = D // 2
     piece = half // 4
     for c in range(4):
@@ -212,11 +250,13 @@
         spread[j * rows : (j + 1) * rows, : I1 // 2] = back[:rows].astype(BF16)
         spread[j * rows : (j + 1) * rows, I1 // 2 :] = back[rows:].astype(BF16)
 
+    if devices > 2:
+        shares.move(2)
     for k in range(1, groups):
         factor_copy(k, mate(k)).wait_recv()
     mask = mask_ref[...]
     for h in range(heads):
-        factor = jnp.concatenate([factors[s, h] for s in range(groups)], axis=0)
+        factor = stack_factors(factors, h)
         for j0 in range(0, J1, 4):
             part = nt_dot(spread[j0 * rows : (j0 + 4) * rows, :], factor)
             for j in range(4):
@@ -224,8 +264,8 @@
                 inner[j0 + j, h * rows : (h + 1) * rows, :] = own.astype(BF16)
     factors_out[...] = factors[...]
 
-    for k in range(1, devices):
-        block_copy(k, peer(k)).wait_recv()
+    for hop in range(3, devices):
+        shares.move(hop)
 
     def store(col, size, value):
         table[:, col : col + size] = value.astype(BF16)
@@ -250,9 +290,9 @@
         row_copy(k, peer(k)).wait_recv()
     rows_out[...] = arriving[...]
     for k in range(1, devices):
-        hidden_copy(k, me).wait_send()
-        block_copy(k, me).wait_send()
         row_copy(k, me).wait_send()
+    features.finish()
+    shares.finish()
     for k in range(1, groups):
         hop_copy(k, dp).wait_send()
         factor_copy(k, dp).wait_send()
@@ -260,7 +300,7 @@
 
 def front(hidden, gain, factors, shared, mask, w_query, w_keyval, devices):
     rows, lanes = mask.shape
-    groups, heads = factors.shape[:2]
+    groups = factors.shape[0]
     slots, width = shared.shape[1:]
     q_cols, kv_cols = w_query.shape[1], w_keyval.shape[1]
     cols = q_cols + kv_cols
@@ -286,18 +326,18 @@
             pltpu.VMEM((rows, D), BF16),
             pltpu.VMEM((D // 2, 2 * rows), F32),
             pltpu.VMEM((J1 * rows, I1), BF16),
-            pltpu.VMEM((J1, heads * rows, lanes), BF16),
+            pltpu.VMEM((J1, factors.shape[2] * rows, lanes), BF16),
             pltpu.VMEM((lanes, J1 * HD), BF16),
             pltpu.VMEM((devices, rows // devices, cols), BF16),
             pltpu.VMEM((devices, rows // devices, cols), BF16),
             pltpu.SemaphoreType.DMA((2, chunks)),
-            pltpu.SemaphoreType.DMA((devices,)),
+            pltpu.SemaphoreType.DMA((2, devices)),
             pltpu.SemaphoreType.DMA((devices,)),
             pltpu.SemaphoreType.DMA((groups,)),
             pltpu.SemaphoreType.DMA((groups,)),
             pltpu.SemaphoreType.DMA((groups,)),
             pltpu.SemaphoreType.DMA((groups,)),
-            pltpu.SemaphoreType.DMA((devices,)),
+            pltpu.SemaphoreType.DMA((2, devices)),
             pltpu.SemaphoreType.DMA((devices,)),
             pltpu.SemaphoreType.DMA((devices,)),
             pltpu.SemaphoreType.DMA((devices,)),
@@ -514,11 +554,8 @@
             turned[b, col : col + size, :] = value[b * HD : (b + 1) * HD].T
 
     expand_shared(shared_ref, RANK * J1 * HD, lanes, store)
-    sources, depth = factor_ref.shape[0], factor_ref.shape[2]
     for h in range(heads):
-        for s in range(sources):
-            first = h * lanes + s * depth
-            factors[first : first + depth, :] = factor_ref[s, h]
+        factors[h * lanes : (h + 1) * lanes, :] = stack_factors(factor_ref, h)
     got_att[me] = att_ref[me]
     for k in range(1, devices):
         att_arrival(k).wait_recv()
@@ -633,8 +670,7 @@
     )
     lanes = groups * slots * RANK * 2
     picked = pick_tenants(jnp.maximum(outgoing, 0), adapter_heads)
-    picked = picked.reshape(groups, slots, heads_here, RANK * 2, I1).transpose(0, 2, 1, 3, 4)
-    picked = picked.reshape(groups, heads_here, slots * RANK * 2, I1)
+    picked = picked.reshape(groups, slots, heads_here, RANK * 2, I1)
 
     incoming = lax.dynamic_index_in_dim(tenant_lists, dp, 1, keepdims=False)
     ids = jnp.where(incoming >= 0, jnp.arange(groups, dtype=jnp.int32)[:, None] * stored + incoming, -1)

time: 152 us -> 140 us (0.921)
  Pallas kernels: 129 us -> 121 us
  local copies, waits for them, and re-layouts: 18.4 us -> 15.1 us
    pallas_call x1, Pallas kernels: 58.2 us -> 46.4 us  [front(): pl.pallas_call(functools.partial(front_kernel, devices, groups), in_specs...]
    pallas_call x1, Pallas kernels: 37.7 us -> 46 us  [project_out(): pl.pallas_call(functools.partial(output_kernel, devices), in_specs=[vmem,...]
    pallas_call x1, Pallas kernels: 28.6 us -> 24.1 us  [attend(): pl.pallas_call(functools.partial(attend_kernel, slots), in_specs=[pl.Bloc...]
    reshape x2 -> x1, local copies, waits for them, and re-layouts: 7.3 us -> 4.1 us  [on_device(): picked = picked.reshape(groups, slots, heads_here, RANK * 2, I1)]
where the time goes in v4:
time: 140 us; the launch traced here: 139 us
  Pallas kernels  121 us (86%)
  local copies, waits for them, and re-layouts  15.1 us (11%)
  other arithmetic  1.88 us (1%)
    pallas_call x1, Pallas kernels, front(): pl.pallas_call(functools.partial(front_kernel, devices, groups), in_specs...  46.4 us
    pallas_call x1, Pallas kernels, project_out(): pl.pallas_call(functools.partial(output_kernel, devices), in_specs=[vmem,...  46 us
    pallas_call x1, Pallas kernels, attend(): pl.pallas_call(functools.partial(attend_kernel, slots), in_specs=[pl.Bloc...  24.1 us
    pallas_call x1, Pallas kernels, pick_tenants(): pl.pallas_call(functools.partial(pick_kernel, count), in_specs=[pl.BlockS...  4.27 us
    reshape x1, local copies, waits for them, and re-layouts, on_device(): picked = picked.reshape(groups, slots, heads_here, RANK * 2, I1)  4.1 us

profile of v4, /device:TPU:9, one launch (start us, length us, event | category | flops | bytes accessed | tf_op | source)
XLA Modules:
  0.0 139.0 jit_solution(16657558505391971422)
XLA Ops:
  0.0 0.0 copy-start
  0.0 1.4 dynamic_slice.11.length_ref
  1.4 0.1 add.38
  1.5 0.1 add.39
  1.5 0.7 dynamic-slice_reduce_fusion
  2.3 0.1 squeeze.6
  2.3 0.7 constant_dynamic-slice_fusion
  3.0 0.1 reshape.58
  3.1 0.5 compare_select_fusion
  3.6 0.1 broadcast_in_dim.12
  3.7 0.1 eq.52
  3.8 1.4 reshape.57.gain_ref
  5.1 1.4 fusion.2
  6.5 0.0 copy-done
  6.5 1.2 fusion.shared_ref
  7.7 4.3 %shard_map.109 = bf16[32,8,4,2,512]{4,3,2,1,0:T(2,128)(2,1)} custom-call(s32[32]{0:T(128)} %get-tuple-element.14.index_ref, bf16[200,8,4,2,512]{4,3,2,1,0:T(2,128)(2,1)} %store_ref.1), custom_call_target="tpu_custom_call" | custom-call | tf_op jit(solution)/shard_map/pallas_call | solution.py:43
  11.9 4.1 %reshape.59.factor_ref = bf16[4,8,8,8,512]{4,3,2,1,0:T(8,128)(2,1)} reshape(bf16[32,8,4,2,512]{4,3,2,1,0:T(2,128)(2,1)} %shard_map.109) | data formatting | bytes 4194304 | tf_op jit(solution)/shard_map/reshape | solution.py:673
  16.1 46.4 %shard_map.110 = (bf16[4,8,8,8,512]{4,3,2,1,0:T(8,128)(2,1)}, bf16[4,32,4096]{2,1,0:T(8,128)(2,1)}, bf16[4,16,1280]{2,1,0:T(8,128)(2,1)}) custom-call(bf16[64,2048]{1,0:T(8,128)(2,1)} %hidden_ref.1, bf16[1,8192]{1,0:T(2,128)(2,1)} %reshape.57.gain_ref, bf16[4,8,8,8,512]{4,3,2,1,0:T(8,128)(2,1)} %reshape.59.factor_ref, bf16[4,8,4096]{2,1,0:T(8,128)(2,1)} %fusion.shared_ref, ...), custom_call_target="tpu_custom_call" | custom-call | tf_op jit(solution)/shard_map/pallas_call | solution.py:310
  62.4 0.8 slice_bitcast_fusion.1
  63.2 0.9 slice_bitcast_fusion
  64.1 0.1 copy.15
  64.2 0.7 reshape.61.query_ref
  65.0 0.6 reshape.62.fresh_ref
  65.6 24.1 %shard_map.111 = bf16[16,32,128]{2,1,0:T(8,128)(2,1)} custom-call(s32[16]{0:T(128)} %dynamic_slice.11.length_ref, bf16[16,32,128]{2,1,0:T(8,128)(2,1)} %reshape.61.query_ref, bf16[16,8,128]{2,1,0:T(8,128)(2,1)} %reshape.62.fresh_ref, bf16[16,2048,1024]{2,1,0:T(8,128)(2,1)} %bitcast.3.cache_ref), custom_call_target="tpu_custom_call" | custom-call | flops 536870912 | bytes 33554432 | tf_op jit(solution)/shard_map/pallas_call | solution.py:439
  89.7 1.6 %copy.17 = bf16[16,32,128]{2,0,1:T(8,128)(2,1)} copy(bf16[16,32,128]{2,1,0:T(8,128)(2,1)} %shard_map.111) | data formatting | bytes 262144 | tf_op jit(solution)/shard_map/pallas_call | solution.py:439
  91.3 46.0 %shard_map.112 = bf16[64,2048]{1,0:T(8,128)(2,1)} custom-call(bf16[4,8,16,128]{3,2,1,0:T(8,128)(2,1)} %bitcast.11, bf16[4,8,8,8,512]{4,3,2,1,0:T(8,128)(2,1)} %get-tuple-element.9.factor_ref, bf16[4,32,4096]{2,1,0:T(8,128)(2,1)} %get-tuple-element.10.shared_ref, f32[64,256]{1,0:T(8,128)} %get-tuple-element.11.mask_ref, bf16[1024,8192]{1,0:T(8,128)(2,1)} %weight_ref.1), custom_call_target="tpu_custom_call" | custom-call | tf_op jit(solution)/shard_map/pallas_call | solution.py:621
  137.3 1.7 %copy.19 = bf16[64,2048]{1,0:T(8,128)(2,1)} copy(bf16[64,2048]{1,0:T(8,128)(2,1)} %shard_map.112) | data formatting | bytes 524288
  (3 shorter events, 0.0 us)
Async XLA Ops:
  0.0 6.5 %copy-start = (bf16[200,4096]{1,0:T(8,128)(2,1)S(1)}, bf16[200,4096]{1,0:T(8,128)(2,1)}, u32[]{:S(2)}) copy-start(bf16[200,4096]{1,0:T(8,128)(2,1)} %param.21) | copy-start | bytes 4915204
